TPU v7x, 32 devices: a whole 2x2x4 slice. The times are simulated.
32 devices in a mesh: groups: 2 (over x), lon: 16 (over z, y, core).
Axes of the slice: x: 2, y: 2, z: 4, core: 2. Of those that a mesh axis runs over, the one named last changes fastest.
Arguments:
- observations: bfloat16 [32768, 128], P(('groups', 'lon')), parts along dimension 0, may hold values from -6 to 6
- cell_index: int32 [32768], P(('groups', 'lon')), parts along dimension 0, may hold values from 0 to 1023
- tile_counts: int32 [32, 16], P(('groups', 'lon')), parts along dimension 0, may hold values from 0 to 128, as said below
- enc_weight: bfloat16 [128, 384], replicated, may hold values from -0.5 to 0.5
- conv_weight: bfloat16 [3, 3, 384, 384], replicated, may hold values from -0.109375 to 0.109375
- cotangent: bfloat16 [128, 256, 384], P('groups', 'lon'), parts along dimension 0, may hold values from -6 to 6
Outputs:
- features: bfloat16 [128, 256, 384], P('groups', 'lon'), parts along dimension 0
- obs_grad: bfloat16 [32768, 128], P(('groups', 'lon')), parts along dimension 0
- conv_grad: bfloat16 [6, 3, 384, 384], P('groups'), parts along dimension 0
- enc_grad: bfloat16 [256, 384], P('groups'), parts along dimension 0
There are 2 independent parts, one for each index of `groups`. A program takes and returns all parts, laid end to end along the dimension named above; an argument that names none is the same for every part. Nothing has to cross between parts.
Inputs may be any that keep to these rules, and one draw needn't show every extreme that they name: `tile_counts`: each row sums to 1024; the observations of device s come in runs by destination tile in ascending order with these lengths; in every draw one tile receives exactly 128 observations from every device.
All inputs are finite; a program needn't handle non-finite values.
Results may differ from a plain program's by a relative error of at most 0.0054.
Values may be sent and summed in bfloat16 or wider, within the bound.
A program may use at most 128 MiB of HBM per device.

v0:
```python
import jax
import jax.numpy as jnp
from jax import lax
from jax.sharding import PartitionSpec as P


def padded(x, sides, width):
    for axis, dim in sides:
        peers, length = (lax.axis_size(axis), x.shape[dim])
        up = [(i, (i + 1) % peers) for i in range(peers)]
        down = [(j, i) for i, j in up]
        last = lax.slice_in_dim(x, length - width, length, axis=dim)
        first = lax.slice_in_dim(x, 0, width, axis=dim)
        before = lax.ppermute(last, axis, up)
        after = lax.ppermute(first, axis, down)
        x = jnp.concatenate([before, x, after], axis=dim)
    return x


def logistic_grad(pre):
    sig = jax.nn.sigmoid(pre)
    return sig * (1.0 + pre * (1.0 - sig))


def pad_lat(grid):
    return jnp.pad(grid, ((1, 1), (0, 0), (0, 0)))


def per_device(observations, cell_index, tile_counts, enc_weight, conv_weight, cotangent):
    lat_rows, lon_cols, chans = cotangent.shape
    obs_dev, feats = observations.shape
    ntiles = lax.axis_size("lon")
    cap = 2 * obs_dev // ntiles
    ncell = lat_rows * lon_cols
    counts = tile_counts[0]
    inclusive = jnp.cumsum(counts)
    offsets = inclusive - counts
    slot = jnp.arange(cap, dtype=jnp.int32)
    source_idx = offsets[:, None] + slot[None, :]
    valid = slot[None, :] < counts[:, None]
    safe_idx = jnp.clip(source_idx, 0, obs_dev - 1)
    send_rows = jnp.where(valid[:, :, None], observations[safe_idx], jnp.zeros((), jnp.bfloat16))
    send_cells = jnp.where(valid, cell_index[safe_idx], -1)
    recv_rows = lax.all_to_all(send_rows, "lon", split_axis=0, concat_axis=0, tiled=True)
    recv_cells = lax.all_to_all(send_cells, "lon", split_axis=0, concat_axis=0, tiled=True)
    total = ntiles * cap
    block = min(512, total)
    nblock = total // block
    rows_blocks = recv_rows.reshape(nblock, block, feats)
    cell_blocks = recv_cells.reshape(nblock, block)
    cell_ids = jnp.arange(ncell, dtype=jnp.int32)

    def spread(carry, blk):
        sums, numbers = carry
        rows_b, cells_b = blk
        match = cells_b[:, None] == cell_ids[None, :]
        onehot = match.astype(jnp.bfloat16)
        sums = sums + lax.dot_general(
            onehot, rows_b, (((0,), (0,)), ((), ())), preferred_element_type=jnp.float32
        )
        numbers = numbers + jnp.sum(match.astype(jnp.int32), axis=0)
        return ((sums, numbers), None)

    init = (jnp.zeros((ncell, feats), jnp.float32), jnp.zeros((ncell,), jnp.int32))
    (raw_sum, count), _ = lax.scan(spread, init, (rows_blocks, cell_blocks))
    denom = jnp.maximum(count, 1).astype(jnp.float32)[:, None]
    raw_mean = (raw_sum / denom).astype(jnp.bfloat16)
    pre = jnp.dot(raw_mean, enc_weight, preferred_element_type=jnp.float32)
    encoded = jax.nn.silu(pre).astype(jnp.bfloat16).reshape(lat_rows, lon_cols, chans)
    xpad = pad_lat(padded(encoded, (("lon", 1),), 1))
    gpad = pad_lat(padded(cotangent, (("lon", 1),), 1))
    cot_flat = cotangent.reshape(-1, chans)
    out = jnp.zeros((ncell, chans), jnp.float32)
    d_enc = jnp.zeros((ncell, chans), jnp.float32)
    taps = []
    for lat_tap in range(3):
        row_taps = []
        for lon_tap in range(3):
            window = xpad[lat_tap : lat_tap + lat_rows, lon_tap : lon_tap + lon_cols].reshape(
                -1, chans
            )
            out = out + jnp.dot(
                window, conv_weight[lat_tap, lon_tap], preferred_element_type=jnp.float32
            )
            back = gpad[
                2 - lat_tap : 2 - lat_tap + lat_rows, 2 - lon_tap : 2 - lon_tap + lon_cols
            ].reshape(-1, chans)
            d_enc = d_enc + lax.dot_general(
                back,
                conv_weight[lat_tap, lon_tap],
                (((1,), (1,)), ((), ())),
                preferred_element_type=jnp.float32,
            )
            row_taps.append(
                lax.dot_general(
                    window, cot_flat, (((0,), (0,)), ((), ())), preferred_element_type=jnp.float32
                )
            )
        taps.append(jnp.stack(row_taps))
    conv_raw = jnp.stack(taps)
    features = out.astype(jnp.bfloat16).reshape(lat_rows, lon_cols, chans)
    d_pre = (d_enc * logistic_grad(pre)).astype(jnp.bfloat16)
    enc_raw = lax.dot_general(
        raw_mean, d_pre, (((0,), (0,)), ((), ())), preferred_element_type=jnp.float32
    )
    d_raw = lax.dot_general(
        d_pre, enc_weight, (((1,), (1,)), ((), ())), preferred_element_type=jnp.float32
    )
    cell_grad = (d_raw / denom).astype(jnp.bfloat16)

    def pick(cells_b):
        onehot = (cells_b[:, None] == cell_ids[None, :]).astype(jnp.bfloat16)
        return jnp.dot(onehot, cell_grad, preferred_element_type=jnp.float32).astype(jnp.bfloat16)

    slot_grads = lax.map(pick, cell_blocks).reshape(ntiles, cap, feats)
    back_rows = lax.all_to_all(slot_grads, "lon", split_axis=0, concat_axis=0, tiled=True).reshape(
        total, feats
    )
    position = jnp.arange(obs_dev, dtype=jnp.int32)
    dest = jnp.sum((position[:, None] >= inclusive[None, :]).astype(jnp.int32), axis=1)
    tile_ids = jnp.arange(ntiles, dtype=jnp.int32)
    start_of = jnp.sum(jnp.where(dest[:, None] == tile_ids[None, :], offsets[None, :], 0), axis=1)
    obs_grad = back_rows[dest * cap + position - start_of]
    conv_flat = conv_raw.reshape(-1)
    enc_flat = enc_raw.reshape(-1)
    conv_sum, enc_sum = lax.psum((conv_flat, enc_flat), "lon")
    norm = jnp.sqrt(jnp.sum(conv_sum * conv_sum) + jnp.sum(enc_sum * enc_sum))
    scale = jnp.minimum(1.0, 1.0 / (norm + 1e-06))
    conv_out = (conv_sum * scale).astype(jnp.bfloat16)
    enc_out = (enc_sum * scale).astype(jnp.bfloat16)
    return (features, obs_grad, conv_out.reshape(conv_raw.shape), enc_out.reshape(enc_raw.shape))


def solution(mesh):
    return jax.shard_map(
        per_device,
        mesh=mesh,
        in_specs=(
            P(("groups", "lon"), None),
            P(("groups", "lon")),
            P(("groups", "lon"), None),
            P(),
            P(),
            P("groups", "lon", None),
        ),
        out_specs=(
            P("groups", "lon", None),
            P(("groups", "lon"), None),
            P("groups", None, None, None),
            P("groups", None),
        ),
        check_vma=False,
    )
```

profile of v0, /device:TPU:0, one launch (start us, length us, event | category | flops | bytes accessed | tf_op | source)
XLA Modules:
  0.0 273.6 jit_solution(5577552491315683740)
XLA Ops:
  7.2 0.8 copy.72
  8.9 8.6 %gather_fusion = s32[2048]{0:T(1024)S(1)} fusion(s32[1024]{0:T(1024)S(1)} %copy-done.2, s32[2048]{0:T(1024)S(1)} %fusion.91), kind=kCustom, calls=%fused_computation | custom fusion | bytes 24576 | tf_op jit(solution)/shard_map/gather | solution.py:43
  18.2 7.4 %all-to-all-start = ((s32[16,1,128]{2,1,0:T(1,128)}), s32[16,1,128]{2,1,0:T(1,128)}, u32[]{:S(2)}, u32[]{:S(2)}) async-start(s32[16,1,128]{2,1,0:T(1,128)} %compare_select_fusion), calls=%async_computation | async-start | bytes 16384 | tf_op jit(solution)/shard_map/all_to_all | solution.py:45
  25.6 1.9 fusion.103
  27.6 4.3 %collective-permute-start.3 = (bf16[64,1,384]{2,1,0:T(2,128)(2,1)}, bf16[64,1,384]{2,1,0:T(2,128)(2,1)S(1)}, u32[]{:S(2)}, u32[]{:S(2)}) collective-permute-start(bf16[64,1,384]{2,1,0:T(2,128)(2,1)} %get-tuple-element.132), channel_id=1, source_target_pairs={{1,0},{2,1},{3,2},{4,3},{5,4},{6,5},{7,6},{8,7},{9,8},{10,9},{11,1... | collective-permute-start | bytes 147464 | tf_op jit(solution)/shard_map/ppermute | solution.py:15
  32.6 6.2 %gather_fusion.1 = bf16[2048,128]{1,0:T(8,128)(2,1)S(1)} fusion(bf16[1024,128]{1,0:T(8,128)(2,1)S(1)} %copy-done, s32[2048]{0:T(1024)S(1)} %fusion.91), kind=kCustom, calls=%fused_computation.1 | custom fusion | bytes 1056768 | tf_op jit(solution)/shard_map/gather | solution.py:42
  38.8 0.8 select_reduce_fusion
  39.6 1.1 broadcast_select_fusion
  40.8 1.8 fusion.44
  43.2 5.8 %all-to-all-start.1 = ((bf16[16,128,128]{2,1,0:T(8,128)(2,1)}), bf16[16,128,128]{2,1,0:T(8,128)(2,1)S(1)}, u32[]{:S(2)}, u32[]{:S(2)}) async-start(bf16[16,128,128]{2,1,0:T(8,128)(2,1)} %broadcast_select_fusion), calls=%async_computation.1 | async-start | bytes 1048576 | tf_op jit(solution)/shard_map/all_to_all | solution.py:44
  49.6 1.4 reduce.5
  51.0 1.9 fusion.23
  53.4 1.8 fusion.30
  55.2 1.8 fusion.34
  57.0 1.9 fusion.38
  58.9 2.6 pad_maximum_fusion.1
  61.5 1.8 fusion.48
  63.3 1.9 fusion.52
  65.1 1.8 fusion.60
  66.9 1.8 fusion.56
  68.8 11.0 %while.25 = (s32[]{:T(128)}, f32[1024,128]{1,0:T(8,128)}, s32[1024]{0:T(1024)S(1)}, s32[4,512]{1,0:T(4,128)S(1)}, bf16[4,512,128]{2,1,0:T(8,128)(2,1)S(1)}, /*index=5*/s32[]{:T(128)}, s32[]{:T(128)}) while((s32[]{:T(128)}, f32[1024,128]{1,0:T(8,128)}, s32[1024]{0:T(1024)S(1)}, s32[4,512]{1,0:T(4,128)S(1)}, ...), condition=%wide.region_3.4_spmd.clone, body=%wide.region_1.3_spmd.clone.sunk | while | flops 136578048 | bytes 1204328 | solution.py:65
  68.8 1.7 fusion.140
  70.8 2.7 fusion.140
  73.8 2.7 fusion.140
  76.8 2.7 fusion.140
  79.9 1.7 multiply_convert_fusion.2
  81.6 1.8 fusion.46
  85.1 4.4 %collective-permute-start.1 = (bf16[64,1,384]{2,0,1:T(8,128)(2,1)}, bf16[64,1,384]{2,0,1:T(8,128)(2,1)S(1)}, u32[]{:S(2)}, u32[]{:S(2)}) collective-permute-start(bf16[64,1,384]{2,0,1:T(8,128)(2,1)} %get-tuple-element.136), channel_id=1, source_target_pairs={{1,0},{2,1},{3,2},{4,3},{5,4},{6,5},{7,6},{8,7},{9,8},{10,9},{11,1... | collective-permute-start | bytes 147464 | tf_op jit(solution)/shard_map/ppermute | solution.py:15
  89.6 1.3 multiply_convert_fusion.1
  90.9 0.9 copy-done.26
  92.2 7.6 %while.24 = (s32[]{:T(128)}, bf16[4,512,128]{2,1,0:T(8,128)(2,1)}, s32[4,512]{1,0:T(4,128)}, bf16[1024,128]{1,0:T(8,128)(2,1)S(1)}, s32[]{:T(128)}) while((s32[]{:T(128)}, bf16[4,512,128]{2,1,0:T(8,128)(2,1)}, s32[4,512]{1,0:T(4,128)}, bf16[1024,128]{1,0:T(8,128)(2,1)S(1)}, s32[]{:T(128)}) %tuple.68), condition=%wide.region_5.6_spmd.clone, body=%wide.region_4.5_spmd.clone.sunk | while | flops 134807552 | bytes 399437 | solution.py:115
  92.2 0.8 constant_dynamic-slice_fusion.4
  92.9 1.2 fusion.138
  94.8 1.2 fusion.138
  96.7 1.2 fusion.138
  98.6 1.2 fusion.138
  100.4 5.9 %all-to-all-start.2 = ((bf16[16,128,128]{2,1,0:T(8,128)(2,1)}), bf16[16,128,128]{2,1,0:T(8,128)(2,1)S(1)}, u32[]{:S(2)}, u32[]{:S(2)}) async-start(bf16[16,128,128]{2,1,0:T(8,128)(2,1)} %bitcast.34), calls=%async_computation.2 | async-start | bytes 1048576 | tf_op jit(solution)/shard_map/all_to_all | solution.py:116
  107.1 1.5 fusion.29
  112.3 0.8 constant_dynamic-update-slice_fusion.1
  115.6 2.8 %pad_maximum_fusion = f32[3,3,384,384]{3,2,1,0:T(8,128)} fusion(f32[1,3,384,384]{3,2,1,0:T(8,128)S(1)} %maximum_bitcast_fusion.2, f32[1,3,384,384]{3,2,1,0:T(8,128)S(1)} %get-tuple-element.140, f32[1,3,384,384]{3,2,1,0:T(8,128)S(1)} %get-tuple-element.139), kind=kLoop, calls=%fused_computation.23 | loop fusion | flops 2654208 | bytes 10616832 | tf_op jit(solution)/shard_map/stack | solution.py:100
  118.4 6.6 %reshape.290 = f32[1327104]{0:T(1024)} reshape(f32[3,3,384,384]{3,2,1,0:T(8,128)} %pad_maximum_fusion) | data formatting | bytes 10616832 | tf_op jit(solution)/shard_map/reshape | solution.py:124
  129.1 0.8 copy-done.4
  136.7 1.8 add_convert_fusion
  138.5 4.3 %gather_fusion.2 = bf16[1024,128]{1,0:T(8,128)(2,1)} fusion(bf16[2048,128]{1,0:T(8,128)(2,1)S(1)} %bitcast.166, s32[1024]{0:T(1024)S(1)} %copy-done.30), kind=kCustom, calls=%fused_computation.2 | custom fusion | bytes 528384 | tf_op jit(solution)/shard_map/gather | solution.py:123
  142.8 111.9 %all-reduce.5.cloned.1.call-done = (f32[1327104]{0:T(1024)}, f32[49152]{0:T(1024)}) async-done(((f32[1327104]{0:T(1024)}, f32[49152]{0:T(1024)}), (f32[1327104]{0:T(1024)}, f32[49152]{0:T(1024)})) %all-reduce.5.cloned.1.call-update) | async-done | bytes 5505040 | tf_op jit(solution)/shard_map/psum | solution.py:126
  254.7 3.9 %multiply_reduce_fusion = f32[]{:T(128)} fusion(f32[1327104]{0:T(1024)} %get-tuple-element.115), kind=kLoop, calls=%fused_computation.25 | loop fusion | flops 2654207 | bytes 5308420 | tf_op jit(solution)/shard_map/reduce_sum | solution.py:127
  260.6 2.7 multiply_convert_fusion
  263.4 2.6 reshape.292
  (153 shorter events, 28.8 us)
Async XLA Ops:
  7.2 25.4 %copy-start = (bf16[1024,128]{1,0:T(8,128)(2,1)S(1)}, bf16[1024,128]{1,0:T(8,128)(2,1)}, u32[]{:S(2)}) copy-start(bf16[1024,128]{1,0:T(8,128)(2,1)} %param.10) | copy-start | bytes 786436
  7.2 1.7 copy-start.2
  8.9 8.6 %copy-start.31 = (s32[1,16]{1,0:T(1,128)S(1)}, s32[1,16]{1,0:T(1,128)}, u32[]{:S(2)}) copy-start(s32[1,16]{1,0:T(1,128)} %param.12) | copy-start | bytes 196
  18.2 25.0 %all-to-all-start = ((s32[16,1,128]{2,1,0:T(1,128)}), s32[16,1,128]{2,1,0:T(1,128)}, u32[]{:S(2)}, u32[]{:S(2)}) async-start(s32[16,1,128]{2,1,0:T(1,128)} %compare_select_fusion), calls=%async_computation | async-start | bytes 16384 | tf_op jit(solution)/shard_map/all_to_all | solution.py:45
  27.6 23.4 %collective-permute-start.3 = (bf16[64,1,384]{2,1,0:T(2,128)(2,1)}, bf16[64,1,384]{2,1,0:T(2,128)(2,1)S(1)}, u32[]{:S(2)}, u32[]{:S(2)}) collective-permute-start(bf16[64,1,384]{2,1,0:T(2,128)(2,1)} %get-tuple-element.132), channel_id=1, source_target_pairs={{1,0},{2,1},{3,2},{4,3},{5,4},{6,5},{7,6},{8,7},{9,8},{10,9},{11,1... | collective-permute-start | bytes 147464 | tf_op jit(solution)/shard_map/ppermute | solution.py:15
  31.9 19.1 %collective-permute-start.2 = (bf16[64,1,384]{2,1,0:T(2,128)(2,1)}, bf16[64,1,384]{2,1,0:T(2,128)(2,1)}, u32[]{:S(2)}, u32[]{:S(2)}) collective-permute-start(bf16[64,1,384]{2,1,0:T(2,128)(2,1)} %get-tuple-element.131), channel_id=1, source_target_pairs={{0,1},{1,2},{2,3},{3,4},{4,5},{5,6},{6,7},{7,8},{8,9},{9,10},{10,1... | collective-permute-start | bytes 147464 | tf_op jit(solution)/shard_map/ppermute | solution.py:14
  32.6 8.2 %copy-start.3 = (bf16[3,3,384,384]{3,2,1,0:T(8,128)(2,1)S(1)}, bf16[3,3,384,384]{3,2,1,0:T(8,128)(2,1)}, u32[]{:S(2)}) copy-start(bf16[3,3,384,384]{3,2,1,0:T(8,128)(2,1)} %param.14) | copy-start | bytes 7962628
  38.8 2.0 copy-start.5
  43.2 25.6 %all-to-all-start.1 = ((bf16[16,128,128]{2,1,0:T(8,128)(2,1)}), bf16[16,128,128]{2,1,0:T(8,128)(2,1)S(1)}, u32[]{:S(2)}, u32[]{:S(2)}) async-start(bf16[16,128,128]{2,1,0:T(8,128)(2,1)} %broadcast_select_fusion), calls=%async_computation.1 | async-start | bytes 1048576 | tf_op jit(solution)/shard_map/all_to_all | solution.py:44
  57.0 1.9 copy-start.6
  68.8 11.1 %copy-start.34 = (bf16[128,384]{1,0:T(8,128)(2,1)S(1)}, bf16[128,384]{1,0:T(8,128)(2,1)}, u32[]{:S(2)}) copy-start(bf16[128,384]{1,0:T(8,128)(2,1)} %param.13) | copy-start | bytes 294916
  79.8 1.8 copy-start.29
  79.8 11.0 %copy-start.32 = (f32[1024]{0:T(1024)}, f32[1024]{0:T(1024)S(1)}, u32[]{:S(2)}) copy-start(f32[1024]{0:T(1024)S(1)} %maximum_convert_fusion) | copy-start | bytes 12292
  81.6 2.0 copy-start.9
  81.6 2.0 copy-start.7
  83.6 0.9 copy-start.20
  83.6 5.9 %copy-start.12 = (f32[1024,384]{1,0:T(8,128)S(1)}, f32[1024,384]{1,0:T(8,128)}, u32[]{:S(2)}) copy-start(f32[1024,384]{1,0:T(8,128)} %fusion.44) | copy-start | bytes 4718596
  83.6 5.9 %copy-start.13 = (f32[1024,384]{1,0:T(8,128)S(1)}, f32[1024,384]{1,0:T(8,128)}, u32[]{:S(2)}) copy-start(f32[1024,384]{1,0:T(8,128)} %fusion.30) | copy-start | bytes 4718596
  83.6 5.9 %copy-start.14 = (f32[1024,384]{1,0:T(8,128)S(1)}, f32[1024,384]{1,0:T(8,128)}, u32[]{:S(2)}) copy-start(f32[1024,384]{1,0:T(8,128)} %fusion.34) | copy-start | bytes 4718596
  83.6 5.9 %copy-start.15 = (f32[1024,384]{1,0:T(8,128)S(1)}, f32[1024,384]{1,0:T(8,128)}, u32[]{:S(2)}) copy-start(f32[1024,384]{1,0:T(8,128)} %fusion.38) | copy-start | bytes 4718596
  83.6 5.9 %copy-start.16 = (f32[1024,384]{1,0:T(8,128)S(1)}, f32[1024,384]{1,0:T(8,128)}, u32[]{:S(2)}) copy-start(f32[1024,384]{1,0:T(8,128)} %fusion.48) | copy-start | bytes 4718596
  83.6 5.9 %copy-start.17 = (f32[1024,384]{1,0:T(8,128)S(1)}, f32[1024,384]{1,0:T(8,128)}, u32[]{:S(2)}) copy-start(f32[1024,384]{1,0:T(8,128)} %fusion.52) | copy-start | bytes 4718596
  83.7 5.9 %copy-start.18 = (f32[1024,384]{1,0:T(8,128)S(1)}, f32[1024,384]{1,0:T(8,128)}, u32[]{:S(2)}) copy-start(f32[1024,384]{1,0:T(8,128)} %fusion.60) | copy-start | bytes 4718596
  83.7 5.9 %copy-start.19 = (f32[1024,384]{1,0:T(8,128)S(1)}, f32[1024,384]{1,0:T(8,128)}, u32[]{:S(2)}) copy-start(f32[1024,384]{1,0:T(8,128)} %fusion.56) | copy-start | bytes 4718596
  83.7 5.9 %copy-start.21 = (bf16[64,16,384]{2,1,0:T(8,128)(2,1)S(1)}, bf16[64,16,384]{2,1,0:T(8,128)(2,1)}, u32[]{:S(2)}) copy-start(bf16[64,16,384]{2,1,0:T(8,128)(2,1)} %get-tuple-element.129) | copy-start | bytes 2359300
  85.1 21.9 %collective-permute-start.1 = (bf16[64,1,384]{2,0,1:T(8,128)(2,1)}, bf16[64,1,384]{2,0,1:T(8,128)(2,1)S(1)}, u32[]{:S(2)}, u32[]{:S(2)}) collective-permute-start(bf16[64,1,384]{2,0,1:T(8,128)(2,1)} %get-tuple-element.136), channel_id=1, source_target_pairs={{1,0},{2,1},{3,2},{4,3},{5,4},{6,5},{7,6},{8,7},{9,8},{10,9},{11,1... | collective-permute-start | bytes 147464 | tf_op jit(solution)/shard_map/ppermute | solution.py:15
  89.5 17.6 %collective-permute-start = (bf16[64,1,384]{2,0,1:T(8,128)(2,1)}, bf16[64,1,384]{2,0,1:T(8,128)(2,1)}, u32[]{:S(2)}, u32[]{:S(2)}) collective-permute-start(bf16[64,1,384]{2,0,1:T(8,128)(2,1)} %get-tuple-element.135), channel_id=1, source_target_pairs={{0,1},{1,2},{2,3},{3,4},{4,5},{5,6},{6,7},{7,8},{8,9},{9,10},{10,1... | collective-permute-start | bytes 147464 | tf_op jit(solution)/shard_map/ppermute | solution.py:14
  90.8 0.9 copy-start.26
  91.7 8.0 %copy-start.35 = (f32[1024,128]{1,0:T(8,128)S(1)}, f32[1024,128]{1,0:T(8,128)}, u32[]{:S(2)}) copy-start(f32[1024,128]{1,0:T(8,128)} %get-tuple-element.64) | copy-start | bytes 1572868
  92.1 7.6 %copy-start.27 = (bf16[1024,384]{1,0:T(8,128)(2,1)S(1)}, bf16[1024,384]{1,0:T(8,128)(2,1)}, u32[]{:S(2)}) copy-start(bf16[1024,384]{1,0:T(8,128)(2,1)} %copy-done.26) | copy-start | bytes 2359300
  92.2 7.6 %copy-start.33 = (f32[1024]{0:T(1024)S(1)}, f32[1024]{0:T(1024)}, u32[]{:S(2)}) copy-start(f32[1024]{0:T(1024)} %copy-done.32) | copy-start | bytes 12292
  100.3 8.2 %copy-start.8 = (bf16[64,16,384]{2,1,0:T(8,128)(2,1)S(1)}, bf16[64,16,384]{2,1,0:T(8,128)(2,1)}, u32[]{:S(2)}) copy-start(bf16[64,16,384]{2,1,0:T(8,128)(2,1)} %param.15) | copy-start | bytes 2359300
  100.4 38.1 %all-to-all-start.2 = ((bf16[16,128,128]{2,1,0:T(8,128)(2,1)}), bf16[16,128,128]{2,1,0:T(8,128)(2,1)S(1)}, u32[]{:S(2)}, u32[]{:S(2)}) async-start(bf16[16,128,128]{2,1,0:T(8,128)(2,1)} %bitcast.34), calls=%async_computation.2 | async-start | bytes 1048576 | tf_op jit(solution)/shard_map/all_to_all | solution.py:116
  106.3 148.4 %all-reduce.5.cloned.1.call-start = ((), (), s32[]{:S(2)}) async-start(), calls=%async_computation.3 | async-start | bytes 11010048 | tf_op jit(solution)/shard_map/psum | solution.py:126
  111.6 1.4 copy-start.10
  113.4 1.2 copy-start.24
  113.5 1.0 copy-start.22
  125.1 1.2 copy-start.25
  128.2 1.8 copy-start.4
  133.1 1.2 copy-start.23
  135.2 1.4 copy-start.11
  136.7 1.8 copy-start.30
  254.7 3.9 %copy-start.28 = (f32[49152]{0:T(1024)S(1)}, f32[49152]{0:T(1024)}, u32[]{:S(2)}) copy-start(f32[49152]{0:T(1024)} %get-tuple-element.116) | copy-start | bytes 589828
  263.3 3.4 %copy-start.1 = (bf16[1024,128]{1,0:T(8,128)(2,1)S(1)}, bf16[1024,128]{1,0:T(8,128)(2,1)}, u32[]{:S(2)}) copy-start(bf16[1024,128]{1,0:T(8,128)(2,1)} %param.10) | copy-start | bytes 786436
Sparse Core Ops, SparseCore 0:
  125.2 129.4 all-reduce.4
where the time goes:
time: 275 us; the launch traced here: 274 us
  waiting for transfers between devices  112 us (41%)
  local copies, waits for them, and re-layouts  47.2 us (17%)
  matrix products  46.4 us (17%)
  starting transfers between devices  28 us (10%)
  other arithmetic  23.7 us (9%)
  between operations  16.2 us (6%)
    psum x1, waiting for transfers between devices, per_device(): conv_sum, enc_sum = lax.psum((conv_flat, enc_flat), 'lon')  112 us
    dot_general x9, matrix products, per_device(): lax.dot_general(back, conv_weight[lat_tap, lon_tap], (((1,), (1,)), ((),...  15.9 us
    dot_general x4, matrix products, spread(): lax.dot_general(onehot, rows_b, (((0,), (0,)), ((), ())), preferred_eleme...  9.73 us
    ppermute x2, starting transfers between devices, padded(): after = lax.ppermute(first, axis, down)  8.71 us
    gather x1, local copies, waits for them, and re-layouts, per_device(): send_cells = jnp.where(valid, cell_index[safe_idx], -1)  8.58 us
    dot_general x9, matrix products, per_device(): jnp.dot(window, conv_weight[lat_tap, lon_tap], preferred_element_type=jnp...  7.96 us
    all_to_all x1, starting transfers between devices, per_device(): lax.all_to_all(send_cells, 'lon', split_axis=0, concat_axis=0, tiled=True)  7.44 us
    reshape x1, local copies, waits for them, and re-layouts, per_device(): conv_flat = conv_raw.reshape(-1)  6.6 us
  transfers between devices with their start and end apart: 8, of which 1 were waited for; matrix products, arithmetic and copies ran while one was open for 28% of the time, Pallas kernels for 0%

commit v1 on v0

v1 whole, which is shorter than its diff:
```python
import functools

import jax
import jax.numpy as jnp
from jax import lax
from jax.experimental import pallas as pl
from jax.experimental.pallas import tpu as pltpu
from jax.sharding import PartitionSpec as P

F32, BF16 = jnp.float32, jnp.bfloat16
VMEM = pl.BlockSpec(memory_space=pltpu.VMEM)
LIMIT = 48 * 2**20


def dot(a, b):
    return jnp.dot(a, b, preferred_element_type=F32)


def dot_t(a, b):
    return lax.dot_general(a, b, (((1,), (1,)), ((), ())), preferred_element_type=F32)


def encode_kernel(cells_ref, rows_ref, weight_ref, mean_ref, denom_ref, pre_ref, enc_ref, total):
    blocks, width = cells_ref.shape
    ncell, feats = mean_ref.shape
    total[...] = jnp.zeros_like(total)
    ones = jnp.ones((width, feats), BF16)

    def body(i, _):
        ids = lax.broadcasted_iota(jnp.int32, (ncell, width), 0)
        match = (ids == cells_ref[pl.ds(i, 1), :]).astype(F32).astype(BF16)
        rows = rows_ref[pl.ds(pl.multiple_of(i * width, width), width), :]
        total[...] += dot(match, jnp.concatenate([rows, ones], axis=1))
        return 0

    lax.fori_loop(0, blocks, body, 0)
    denom = jnp.maximum(total[:, feats:], 1.0)
    mean = (total[:, :feats] / denom).astype(BF16)
    mean_ref[...] = mean
    denom_ref[...] = denom
    pre = dot(mean, weight_ref[...])
    pre_ref[...] = pre
    enc_ref[...] = (pre * jax.nn.sigmoid(pre)).astype(BF16)


def pick_kernel(cells_ref, grad_ref, out_ref, grad_t):
    blocks, width = cells_ref.shape
    ncell, feats = grad_ref.shape
    grad_t[...] = grad_ref[...].T

    def body(i, _):
        ids = lax.broadcasted_iota(jnp.int32, (ncell, width), 0)
        match = (ids == cells_ref[pl.ds(i, 1), :]).astype(F32).astype(BF16)
        out = dot(grad_t[...], match)
        out_ref[pl.ds(pl.multiple_of(i * width, width), width), :] = out.T.astype(BF16)
        return 0

    lax.fori_loop(0, blocks, body, 0)


def plan(n, need):
    unit = 16 * n
    units = -(-need // unit)
    streams = min(4, units)
    sizes = [unit * (units // streams + (1 if i < units % streams else 0)) for i in range(streams)]
    return sizes


def conv_kernel(
    n, sizes, xb, gb, w, pre_ref, mean_ref, denom_ref, ew_ref,
    feat_ref, cell_ref, sum_ref,
    xt, acc, denc, sbuf, rbuf, rs_send, rs_recv, ag_send, ag_recv,
):
    lane = xb.shape[2]
    lat16 = pre_ref.shape[0]
    cols = (xb.shape[1] - lat16) // 2
    feats = mean_ref.shape[1]
    taps = 9
    me = lax.axis_index("lon")
    levels = n.bit_length() - 1

    def bit_of(k):
        return lax.rem(me // (2**k), 2)

    def partner(k):
        return me + (1 - 2 * bit_of(k)) * (2**k)

    barrier = pltpu.get_barrier_semaphore()
    for k in range(levels):
        pl.semaphore_signal(
            barrier, inc=1, device_id={"lon": partner(k)}, device_id_type=pl.DeviceIdType.MESH
        )
    pl.semaphore_wait(barrier, levels)

    starts, ranges = [], []
    base = 0
    for s, size in enumerate(sizes):
        order = list(range(levels))
        if s % 2 and levels > 2:
            order = [0] + order[2:] + [1]
        off, length, stages = base, size, []
        for k in order:
            half = length // 2
            b = bit_of(k)
            keep = pl.multiple_of(off + b * half, 16)
            send = pl.multiple_of(off + (1 - b) * half, 16)
            stages.append((k, keep, send, half))
            off, length = keep, half
        starts.append(base)
        ranges.append(stages)
        base += size
    ends = [a + b for a, b in zip(starts, sizes)]

    copies = []
    pos = [0] * len(sizes)
    flying = [None] * len(sizes)

    def send_sum(s, j):
        k, keep, send, half = ranges[s][j]
        sbuf[pl.ds(send, half), :] = acc[pl.ds(send, half), :].astype(BF16)
        copy = pltpu.make_async_remote_copy(
            src_ref=sbuf.at[pl.ds(send, half), :],
            dst_ref=rbuf.at[pl.ds(keep, half), :],
            send_sem=rs_send.at[s, j], recv_sem=rs_recv.at[s, j],
            device_id={"lon": partner(k)}, device_id_type=pl.DeviceIdType.MESH,
        )
        copy.start()
        copies.append(copy)
        flying[s] = copy

    def send_result(s, j):
        k, keep, send, half = ranges[s][j]
        copy = pltpu.make_async_remote_copy(
            src_ref=sum_ref.at[pl.ds(keep, half), :],
            dst_ref=sum_ref.at[pl.ds(keep, half), :],
            send_sem=ag_send.at[s, j], recv_sem=ag_recv.at[s, j],
            device_id={"lon": partner(k)}, device_id_type=pl.DeviceIdType.MESH,
        )
        copy.start()
        copies.append(copy)
        flying[s] = copy

    def begin(s):
        send_sum(s, 0)

    def step(s):
        p = pos[s]
        if p >= 2 * levels:
            return
        flying[s].wait_recv()
        if p < levels:
            k, keep, send, half = ranges[s][p]
            value = acc[pl.ds(keep, half), :] + rbuf[pl.ds(send, half), :].astype(F32)
            if p + 1 < levels:
                acc[pl.ds(keep, half), :] = value
                send_sum(s, p + 1)
            else:
                sum_ref[pl.ds(keep, half), :] = value.astype(BF16)
                send_result(s, levels - 1)
        else:
            j = 2 * levels - 1 - p
            if j > 0:
                send_result(s, j - 1)
        pos[s] = p + 1

    for b in range(3):
        xt[b] = xb[b, pl.ds(cols, lat16), :].T

    def raw_tap(t, _):
        a, b = t // 3, lax.rem(t, 3)
        grad = gb[1, pl.ds(pl.multiple_of((2 - a) * cols, 16), lat16), :]
        acc[pl.ds(pl.multiple_of(t * lane, 16), lane), :] = dot(xt[b], grad)
        return 0

    tile = min(256, lat16)
    tiles = lat16 // tile

    def denc_tile(r, _):
        total = None
        for t in range(taps):
            a, b = t // 3, t % 3
            rows = gb[2 - b, pl.ds(pl.multiple_of((2 - a) * cols + r * tile, 16), tile), :]
            part = dot_t(rows, w[t * lane : (t + 1) * lane, :])
            total = part if total is None else total + part
        here = pl.ds(pl.multiple_of(r * tile, 16), tile)
        pre = pre_ref[here, :]
        sig = jax.nn.sigmoid(pre)
        d_pre = (total * (sig * (1.0 + pre * (1.0 - sig)))).astype(BF16)
        denc[here, :] = d_pre
        cell_ref[here, :] = (dot_t(d_pre, ew_ref[...]) / denom_ref[here, :]).astype(BF16)
        return 0

    def feat_tile(r, _):
        total = None
        for t in range(taps):
            a, b = t // 3, t % 3
            rows = xb[b, pl.ds(pl.multiple_of(a * cols + r * tile, 16), tile), :]
            part = dot(rows, w[t * lane : (t + 1) * lane, :])
            total = part if total is None else total + part
        feat_ref[pl.ds(pl.multiple_of(r * tile, 16), tile), :] = total.astype(BF16)
        return 0

    last = len(sizes) - 1
    done = 0
    for s in range(last):
        upto = min(taps, -(-ends[s] // lane))
        lax.fori_loop(done, upto, raw_tap, 0)
        done = upto
        begin(s)
    if done < taps:
        lax.fori_loop(done, taps, raw_tap, 0)
    for r in range(0, tiles, 2):
        lax.fori_loop(r, min(r + 2, tiles), denc_tile, 0)
        for s in range(last):
            step(s)
    acc[taps * lane : taps * lane + feats, :] = lax.dot_general(
        mean_ref[...], denc[...], (((0,), (0,)), ((), ())), preferred_element_type=F32
    )
    if taps * lane + feats < base:
        acc[taps * lane + feats : base, :] = jnp.zeros((base - taps * lane - feats, lane), F32)
    begin(last)
    for r in range(0, tiles, 2):
        lax.fori_loop(r, min(r + 2, tiles), feat_tile, 0)
        for s in range(last + 1):
            step(s)
    while min(pos) < 2 * levels:
        for s in range(last + 1):
            step(s)
    for copy in copies:
        copy.wait_send()


def conv_call(n, xb, gb, w, pre, mean, denom, ew):
    lane = xb.shape[2]
    ncell, feats = mean.shape
    need = 9 * lane + feats
    sizes = plan(n, need)
    rows = sum(sizes)
    levels = n.bit_length() - 1
    sems = pltpu.SemaphoreType.DMA((len(sizes), levels))
    return pl.pallas_call(
        functools.partial(conv_kernel, n, sizes),
        out_shape=(
            jax.ShapeDtypeStruct((ncell, lane), BF16),
            jax.ShapeDtypeStruct((ncell, feats), BF16),
            jax.ShapeDtypeStruct((rows, lane), BF16),
        ),
        in_specs=[VMEM] * 7,
        out_specs=(VMEM,) * 3,
        scratch_shapes=[
            pltpu.VMEM((3, lane, ncell), BF16),
            pltpu.VMEM((rows, lane), F32),
            pltpu.VMEM((ncell, lane), BF16),
            pltpu.VMEM((rows, lane), BF16),
            pltpu.VMEM((rows, lane), BF16),
            sems, sems, sems, sems,
        ],
        compiler_params=pltpu.CompilerParams(
            collective_id=0, has_side_effects=True, vmem_limit_bytes=LIMIT
        ),
        name="conv",
    )(xb, gb, w, pre, mean, denom, ew)


def shifted(grid, ntiles):
    up = [(i, (i + 1) % ntiles) for i in range(ntiles)]
    down = [(j, i) for i, j in up]
    before = lax.ppermute(grid[:, -1:], "lon", up)
    after = lax.ppermute(grid[:, :1], "lon", down)
    views = jnp.stack([
        jnp.concatenate([before, grid[:, :-1]], axis=1),
        grid,
        jnp.concatenate([grid[:, 1:], after], axis=1),
    ])
    views = jnp.pad(views, ((0, 0), (1, 1), (0, 0), (0, 0)))
    return views.reshape(3, -1, grid.shape[-1])


def per_device(observations, cell_index, tile_counts, enc_weight, conv_weight, cotangent):
    lat_rows, lon_cols, chans = cotangent.shape
    obs_dev, feats = observations.shape
    ntiles = lax.axis_size("lon")
    cap = 2 * obs_dev // ntiles
    ncell = lat_rows * lon_cols
    total = ntiles * cap
    counts = tile_counts[0]
    inclusive = jnp.cumsum(counts)
    position = jnp.arange(obs_dev, dtype=jnp.int32)
    gaps = cap - counts
    passed = (position[None, :] >= inclusive[:, None]).astype(jnp.int32)
    slot_of = position + jnp.sum(passed * gaps[:, None], axis=0)
    slots = jnp.arange(total, dtype=jnp.int32)
    place = (slots[:, None] == slot_of[None, :]).astype(BF16)
    high, low = cell_index // 16, cell_index % 16
    extra = jnp.stack([high + 1, low], axis=1).astype(BF16)
    sent = dot(
        place, jnp.concatenate([observations, extra, jnp.zeros((obs_dev, feats - 2), BF16)], axis=1)
    ).astype(BF16)
    codes = sent[:, feats : feats + 2].reshape(ntiles, cap, 2).transpose(0, 2, 1)
    codes = jnp.pad(codes, ((0, 0), (0, 14), (0, feats - cap)))
    block = jnp.concatenate([sent[:, :feats].reshape(ntiles, cap, feats), codes], axis=1)
    got = lax.all_to_all(block, "lon", split_axis=0, concat_axis=0, tiled=True)
    recv_rows = got[:, :cap].reshape(total, feats)
    width = min(256, total)
    recv_cells = (
        (got[:, cap, :cap].astype(jnp.int32) - 1) * 16 + got[:, cap + 1, :cap].astype(jnp.int32)
    ).reshape(total // width, width)

    mean, denom, pre, encoded = pl.pallas_call(
        encode_kernel,
        out_shape=(
            jax.ShapeDtypeStruct((ncell, feats), BF16),
            jax.ShapeDtypeStruct((ncell, feats), F32),
            jax.ShapeDtypeStruct((ncell, chans), F32),
            jax.ShapeDtypeStruct((ncell, chans), BF16),
        ),
        in_specs=[VMEM] * 3,
        out_specs=(VMEM,) * 4,
        scratch_shapes=[pltpu.VMEM((ncell, 2 * feats), F32)],
        compiler_params=pltpu.CompilerParams(vmem_limit_bytes=LIMIT),
        name="encode",
    )(recv_cells, recv_rows, enc_weight)

    gb = shifted(cotangent, ntiles)
    xb = shifted(encoded.reshape(lat_rows, lon_cols, chans), ntiles)
    features, cell_grad, sums = conv_call(
        ntiles, xb, gb, conv_weight.reshape(9 * chans, chans), pre, mean, denom, enc_weight
    )
    slot_grads = pl.pallas_call(
        pick_kernel,
        out_shape=jax.ShapeDtypeStruct((total, feats), BF16),
        in_specs=[VMEM] * 2,
        out_specs=VMEM,
        scratch_shapes=[pltpu.VMEM((feats, ncell), BF16)],
        compiler_params=pltpu.CompilerParams(vmem_limit_bytes=LIMIT),
        name="pick",
    )(recv_cells, cell_grad)
    back_rows = lax.all_to_all(
        slot_grads.reshape(ntiles, cap, feats), "lon", split_axis=0, concat_axis=0, tiled=True
    ).reshape(total, feats)
    take = (slot_of[:, None] == slots[None, :]).astype(BF16)
    obs_grad = dot(take, back_rows).astype(BF16)

    sums = sums[: 9 * chans + feats].astype(F32)
    norm = jnp.sqrt(jnp.sum(sums * sums))
    scale = jnp.minimum(1.0, 1.0 / (norm + 1e-06))
    out = (sums * scale).astype(BF16)
    return (
        features.reshape(cotangent.shape),
        obs_grad,
        out[: 9 * chans].reshape(conv_weight.shape),
        out[9 * chans :],
    )


def solution(mesh):
    return jax.shard_map(
        per_device,
        mesh=mesh,
        in_specs=(
            P(("groups", "lon"), None),
            P(("groups", "lon")),
            P(("groups", "lon"), None),
            P(),
            P(),
            P("groups", "lon", None),
        ),
        out_specs=(
            P("groups", "lon", None),
            P(("groups", "lon"), None),
            P("groups", None, None, None),
            P("groups", None),
        ),
        check_vma=False,
    )
```

time: 275 us -> 137 us (0.50)
  waiting for transfers between devices: 112 us -> 23.1 us
  Pallas kernels: 0 us -> 68.8 us
  matrix products: 46.4 us -> 4.9 us
  local copies, waits for them, and re-layouts: 47.2 us -> 5.88 us
  between operations: 16.2 us -> 1.58 us
  other arithmetic: 23.7 us -> 11.7 us
  starting transfers between devices: 28 us -> 20.2 us
    psum x1 -> x0, waiting for transfers between devices: 112 us -> none  [per_device(): conv_sum, enc_sum = lax.psum((conv_flat, enc_flat), 'lon')]
    pallas_call x0 -> x3, Pallas kernels: none -> 68.8 us  [the longest x1 62.5 us: conv_call(): pl.pallas_call(functools.partial(conv_kernel, n, sizes), out_shape=(jax.S...]
    dot_general x38 -> x2, matrix products: 46.4 us -> 4.9 us  [dot(): return jnp.dot(a, b, preferred_element_type=F32)]
    gather x3 -> x0, local copies, waits for them, and re-layouts: 19.1 us -> none  [the longest x1 8.58 us: per_device(): send_cells = jnp.where(valid, cell_index[safe_idx], -1)]
    ppermute x4, waiting for transfers between devices: 0.01 us -> 13.4 us  [the longest x2 13.3 us: shifted(): before = lax.ppermute(grid[:, -1:], 'lon', up)]
    reshape x7 -> x1, local copies, waits for them, and re-layouts: 11.6 us -> 0.22 us  [per_device(): codes = sent[:, feats:feats + 2].reshape(ntiles, cap, 2).transpose(0, 2, 1)]
    all_to_all x3 -> x2, waiting for transfers between devices: 0.01 us -> 9.68 us  [the longest x1 9.68 us: per_device(): lax.all_to_all(slot_grads.reshape(ntiles, cap, feats), 'lon', split_axis=...]
    all_to_all x3 -> x2, starting transfers between devices: 19.2 us -> 11 us  [the longest x1 7.38 us: per_device(): got = lax.all_to_all(block, 'lon', split_axis=0, concat_axis=0, tiled=True)]
  transfers between devices with their start and end apart: 8 -> 6, of which waited for: 1 -> 4; matrix products, arithmetic and copies ran while one was open for 28% -> 6% of each run, Pallas kernels for 0% -> 0%
where the time goes in v1:
time: 137 us; the launch traced here: 136 us
  Pallas kernels  68.8 us (50%)
  waiting for transfers between devices  23.1 us (17%)
  starting transfers between devices  20.2 us (15%)
  other arithmetic  11.7 us (9%)
  local copies, waits for them, and re-layouts  5.88 us (4%)
  matrix products  4.9 us (4%)
  between operations  1.58 us (1%)
    pallas_call x1, Pallas kernels, conv_call(): pl.pallas_call(functools.partial(conv_kernel, n, sizes), out_shape=(jax.S...  62.5 us
    ppermute x2, waiting for transfers between devices, shifted(): before = lax.ppermute(grid[:, -1:], 'lon', up)  13.3 us
    all_to_all x1, waiting for transfers between devices, per_device(): lax.all_to_all(slot_grads.reshape(ntiles, cap, feats), 'lon', split_axis=...  9.68 us
    ppermute x2, starting transfers between devices, shifted(): after = lax.ppermute(grid[:, :1], 'lon', down)  8.7 us
    all_to_all x1, starting transfers between devices, per_device(): got = lax.all_to_all(block, 'lon', split_axis=0, concat_axis=0, tiled=True)  7.38 us
    dot_general x2, matrix products, dot(): return jnp.dot(a, b, preferred_element_type=F32)  4.9 us
    reduce_sum x1, other arithmetic, per_device(): norm = jnp.sqrt(jnp.sum(sums * sums))  3.8 us
    all_to_all x1, starting transfers between devices, per_device(): lax.all_to_all(slot_grads.reshape(ntiles, cap, feats), 'lon', split_axis=...  3.57 us
  transfers between devices with their start and end apart: 6, of which 4 were waited for; matrix products, arithmetic and copies ran while one was open for 6% of the time, Pallas kernels for 0%

profile of v1, /device:TPU:0, one launch (start us, length us, event | category | flops | bytes accessed | tf_op | source)
XLA Modules:
  0.0 136.2 jit_solution(16373346674261572228)
XLA Ops:
  0.6 0.7 subtract_bitcast_fusion
  1.3 0.7 fusion.24
  2.0 0.7 copy.24
  2.8 0.1 reduce
  2.9 0.1 select_reduce_fusion
  3.0 0.2 stack.40
  3.2 0.2 stack.41
  3.4 0.1 pad.33.clone
  3.5 2.7 %fusion.7 = bf16[2048,256]{1,0:T(8,128)(2,1)S(1)} fusion(s32[1024]{0:T(1024)S(1)} %iota_add_fusion, bf16[1024,1]{1,0:T(8,128)(2,1)S(1)} %stack.41, bf16[1024,1]{1,0:T(8,128)(2,1)S(1)} %stack.40, bf16[1024,128]{1,0:T(8,128)(2,1)} %param.6, bf16[256]{0:T(256)(128)(2,1)S(1)} %pad.33.clone), kind=kOutput, calls=%fused_computation.13 | convolution fusion | flops 1078460416 | bytes 1319424 | tf_op jit(solution)/shard_map/dot_general | solution.py:16
  6.2 0.0 copy-start.1
  6.3 0.2 copy.27
  6.5 0.9 fusion.11
  7.4 7.4 %all-to-all-start = ((bf16[16,144,128]{2,1,0:T(8,128)(2,1)}), bf16[16,144,128]{2,1,0:T(8,128)(2,1)S(1)}, u32[]{:S(2)}, u32[]{:S(2)}) async-start(bf16[16,144,128]{2,1,0:T(8,128)(2,1)} %fusion.11), calls=%async_computation | async-start | bytes 1179648 | tf_op jit(solution)/shard_map/all_to_all | solution.py:302
  14.8 0.0 copy-done.1
  14.8 0.2 fusion.29
  15.0 0.5 collective-permute-start.2
  15.4 4.0 %collective-permute-start.3 = (bf16[64,1,384]{2,1,0:T(2,128)(2,1)S(1)}, bf16[64,1,384]{2,1,0:T(2,128)(2,1)S(1)}, u32[]{:S(2)}, u32[]{:S(2)}) collective-permute-start(bf16[64,1,384]{2,1,0:T(2,128)(2,1)S(1)} %get-tuple-element.19), channel_id=1, source_target_pairs={{1,0},{2,1},{3,2},{4,3},{5,4},{6,5},{7,6},{8,7},{9,8},{10,9},{11,1... | collective-permute-start | bytes 147464 | tf_op jit(solution)/shard_map/ppermute | solution.py:269
  19.5 0.3 fusion.30
  19.8 11.6 %collective-permute-done.2 = bf16[64,1,384]{2,1,0:T(2,128)(2,1)S(1)} collective-permute-done((bf16[64,1,384]{2,1,0:T(2,128)(2,1)S(1)}, bf16[64,1,384]{2,1,0:T(2,128)(2,1)S(1)}, u32[]{:S(2)}, u32[]{:S(2)}) %collective-permute-start.2) | collective-permute-done | bytes 49184 | tf_op jit(solution)/shard_map/ppermute | solution.py:268
  31.4 0.3 maximum_bitcast_fusion.2
  31.7 0.0 collective-permute-done.3
  31.7 0.3 maximum_bitcast_fusion.3
  32.0 0.0 copy-start
  32.0 1.6 %select_maximum_fusion = bf16[3,66,16,384]{3,2,1,0:T(8,128)(2,1)} fusion(bf16[1,64,16,384]{3,2,1,0:T(8,128)(2,1)S(1)} %maximum_bitcast_fusion.3, bf16[1,64,16,384]{3,2,1,0:T(8,128)(2,1)S(1)} %bitcast.33, bf16[1,64,16,384]{3,2,1,0:T(8,128)(2,1)S(1)} %maximum_bitcast_fusion.2), kind=kLoop, calls=%fused_computation.14 | loop fusion | flops 14598144 | bytes 4792320 | tf_op jit(solution)/shard_map/stack | solution.py:270
  33.6 0.0 all-to-all-done
  33.7 0.0 copy-done
  33.7 2.9 %encode.1 = (bf16[1024,128]{1,0:T(8,128)(2,1)S(1)}, f32[1024,128]{1,0:T(8,128)S(1)}, f32[1024,384]{1,0:T(8,128)S(1)}, bf16[1024,384]{1,0:T(8,128)(2,1)S(1)}) custom-call(s32[8,256]{1,0:T(8,128)S(1)} %add.45.cells_ref, bf16[2048,128]{1,0:T(8,128)(2,1)S(1)} %bitcast.30, bf16[128,384]{1,0:T(8,128)(2,1)S(1)} %copy-done), custom_call_target="tpu_custom_call" | custom-call | tf_op jit(solution)/shard_map/encode/pallas_call | solution.py:309
  36.6 0.2 fusion.31
  36.8 0.1 collective-permute-start
  36.8 0.4 fusion.32
  37.2 4.7 %collective-permute-start.1 = (bf16[64,1,384]{2,1,0:T(2,128)(2,1)S(1)}, bf16[64,1,384]{2,1,0:T(2,128)(2,1)S(1)}, u32[]{:S(2)}, u32[]{:S(2)}) collective-permute-start(bf16[64,1,384]{2,1,0:T(2,128)(2,1)S(1)} %get-tuple-element.23), channel_id=1, source_target_pairs={{1,0},{2,1},{3,2},{4,3},{5,4},{6,5},{7,6},{8,7},{9,8},{10,9},{11,1... | collective-permute-start | bytes 147464 | tf_op jit(solution)/shard_map/ppermute | solution.py:269
  41.9 1.7 %collective-permute-done = bf16[64,1,384]{2,1,0:T(2,128)(2,1)S(1)} collective-permute-done((bf16[64,1,384]{2,1,0:T(2,128)(2,1)S(1)}, bf16[64,1,384]{2,1,0:T(2,128)(2,1)S(1)}, u32[]{:S(2)}, u32[]{:S(2)}) %collective-permute-start) | collective-permute-done | bytes 49184 | tf_op jit(solution)/shard_map/ppermute | solution.py:268
  43.6 0.4 maximum_bitcast_fusion
  43.9 0.2 collective-permute-done.1
  44.1 0.3 maximum_bitcast_fusion.1
  44.3 0.3 select_maximum_fusion.2
  44.6 62.5 %conv.1 = (bf16[1024,384]{1,0:T(8,128)(2,1)S(1)}, bf16[1024,128]{1,0:T(8,128)(2,1)S(1)}, bf16[3584,384]{1,0:T(8,128)(2,1)}) custom-call(bf16[3,1056,384]{2,1,0:T(8,128)(2,1)S(1)} %bitcast.26, bf16[3,1056,384]{2,1,0:T(8,128)(2,1)} %bitcast.32, bf16[3456,384]{1,0:T(8,128)(2,1)} %bitcast.35, f32[1024,384]{1,0:T(8,128)S(1)} %get-tuple-element.12.pre_ref, ...), custom_call_target="tpu_custom_call" | custom-call | tf_op jit(solution)/shard_map/conv/pallas_call | solution.py:241
  107.2 3.8 %fusion.2 = f32[]{:T(128)} fusion(bf16[3584,384]{1,0:T(8,128)(2,1)} %get-tuple-element.17), kind=kLoop, calls=%fused_computation.8 | loop fusion | flops 4128767 | bytes 2752516 | tf_op jit(solution)/shard_map/reduce_sum | solution.py:345
  111.7 3.4 %pick.1 = bf16[2048,128]{1,0:T(8,128)(2,1)} custom-call(s32[8,256]{1,0:T(8,128)S(1)} %add.45.cells_ref, bf16[1024,128]{1,0:T(8,128)(2,1)S(1)} %get-tuple-element.16.grad_ref), custom_call_target="tpu_custom_call" | custom-call | tf_op jit(solution)/shard_map/pick/pallas_call | solution.py:329
  115.1 3.6 %all-to-all-start.1 = ((bf16[16,128,128]{2,1,0:T(8,128)(2,1)}), bf16[16,128,128]{2,1,0:T(8,128)(2,1)S(1)}, u32[]{:S(2)}, u32[]{:S(2)}) async-start(bf16[16,128,128]{2,1,0:T(8,128)(2,1)} %bitcast.17), calls=%async_computation.1 | async-start | bytes 1048576 | tf_op jit(solution)/shard_map/all_to_all | solution.py:338
  118.7 2.3 %fusion.3 = bf16[3584,384]{1,0:T(8,128)(2,1)S(1)} fusion(bf16[3584,384]{1,0:T(8,128)(2,1)} %get-tuple-element.17, f32[]{:T(128)S(6)} %min.3), kind=kLoop, calls=%fused_computation.9 | loop fusion | flops 4128768 | bytes 5505028 | tf_op jit(solution)/shard_map/convert_element_type | solution.py:347
  121.0 0.7 slice.70
  121.7 1.8 %slice.69 = bf16[3456,384]{1,0:T(8,128)(2,1)} slice(bf16[3584,384]{1,0:T(8,128)(2,1)S(1)} %fusion.3), slice={[0:3456], [0:384]} | slice | bytes 5308416 | tf_op jit(solution)/shard_map/slice | solution.py:351
  123.5 9.7 %all-to-all-done.1 = bf16[16,128,128]{2,1,0:T(8,128)(2,1)S(1)} async-done(((bf16[16,128,128]{2,1,0:T(8,128)(2,1)}), bf16[16,128,128]{2,1,0:T(8,128)(2,1)S(1)}, u32[]{:S(2)}, u32[]{:S(2)}) %all-to-all-start.1) | async-done | bytes 524320 | tf_op jit(solution)/shard_map/all_to_all | solution.py:338
  133.1 2.2 %fusion.9 = bf16[1024,128]{1,0:T(8,128)(2,1)} fusion(bf16[2048,128]{1,0:T(8,128)(2,1)S(1)} %bitcast.38, s32[1024]{0:T(1024)S(1)} %iota_add_fusion), kind=kOutput, calls=%fused_computation.19 | convolution fusion | flops 539099136 | bytes 790528 | tf_op jit(solution)/shard_map/dot_general | solution.py:16
  135.3 0.9 copy.29
  (8 shorter events, 0.2 us)
Async XLA Ops:
  6.2 8.6 %copy-start.1 = (bf16[64,16,384]{2,1,0:T(8,128)(2,1)S(1)}, bf16[64,16,384]{2,1,0:T(8,128)(2,1)}, u32[]{:S(2)}) copy-start(bf16[64,16,384]{2,1,0:T(8,128)(2,1)} %param.11) | copy-start | bytes 2359300
  7.4 26.2 %all-to-all-start = ((bf16[16,144,128]{2,1,0:T(8,128)(2,1)}), bf16[16,144,128]{2,1,0:T(8,128)(2,1)S(1)}, u32[]{:S(2)}, u32[]{:S(2)}) async-start(bf16[16,144,128]{2,1,0:T(8,128)(2,1)} %fusion.11), calls=%async_computation | async-start | bytes 1179648 | tf_op jit(solution)/shard_map/all_to_all | solution.py:302
  15.0 16.4 %collective-permute-start.2 = (bf16[64,1,384]{2,1,0:T(2,128)(2,1)S(1)}, bf16[64,1,384]{2,1,0:T(2,128)(2,1)S(1)}, u32[]{:S(2)}, u32[]{:S(2)}) collective-permute-start(bf16[64,1,384]{2,1,0:T(2,128)(2,1)S(1)} %get-tuple-element.18), channel_id=1, source_target_pairs={{0,1},{1,2},{2,3},{3,4},{4,5},{5,6},{6,7},{7,8},{8,9},{9,10},{10,1... | collective-permute-start | bytes 147464 | tf_op jit(solution)/shard_map/ppermute | solution.py:268
  15.4 16.3 %collective-permute-start.3 = (bf16[64,1,384]{2,1,0:T(2,128)(2,1)S(1)}, bf16[64,1,384]{2,1,0:T(2,128)(2,1)S(1)}, u32[]{:S(2)}, u32[]{:S(2)}) collective-permute-start(bf16[64,1,384]{2,1,0:T(2,128)(2,1)S(1)} %get-tuple-element.19), channel_id=1, source_target_pairs={{1,0},{2,1},{3,2},{4,3},{5,4},{6,5},{7,6},{8,7},{9,8},{10,9},{11,1... | collective-permute-start | bytes 147464 | tf_op jit(solution)/shard_map/ppermute | solution.py:269
  32.0 1.7 %copy-start = (bf16[128,384]{1,0:T(8,128)(2,1)S(1)}, bf16[128,384]{1,0:T(8,128)(2,1)}, u32[]{:S(2)}) copy-start(bf16[128,384]{1,0:T(8,128)(2,1)} %ew_ref.1) | copy-start | bytes 294916
  36.8 6.8 %collective-permute-start = (bf16[64,1,384]{2,1,0:T(2,128)(2,1)S(1)}, bf16[64,1,384]{2,1,0:T(2,128)(2,1)S(1)}, u32[]{:S(2)}, u32[]{:S(2)}) collective-permute-start(bf16[64,1,384]{2,1,0:T(2,128)(2,1)S(1)} %get-tuple-element.22), channel_id=1, source_target_pairs={{0,1},{1,2},{2,3},{3,4},{4,5},{5,6},{6,7},{7,8},{8,9},{9,10},{10,1... | collective-permute-start | bytes 147464 | tf_op jit(solution)/shard_map/ppermute | solution.py:268
  37.2 6.9 %collective-permute-start.1 = (bf16[64,1,384]{2,1,0:T(2,128)(2,1)S(1)}, bf16[64,1,384]{2,1,0:T(2,128)(2,1)S(1)}, u32[]{:S(2)}, u32[]{:S(2)}) collective-permute-start(bf16[64,1,384]{2,1,0:T(2,128)(2,1)S(1)} %get-tuple-element.23), channel_id=1, source_target_pairs={{1,0},{2,1},{3,2},{4,3},{5,4},{6,5},{7,6},{8,7},{9,8},{10,9},{11,1... | collective-permute-start | bytes 147464 | tf_op jit(solution)/shard_map/ppermute | solution.py:269
  115.1 18.0 %all-to-all-start.1 = ((bf16[16,128,128]{2,1,0:T(8,128)(2,1)}), bf16[16,128,128]{2,1,0:T(8,128)(2,1)S(1)}, u32[]{:S(2)}, u32[]{:S(2)}) async-start(bf16[16,128,128]{2,1,0:T(8,128)(2,1)} %bitcast.17), calls=%async_computation.1 | async-start | bytes 1048576 | tf_op jit(solution)/shard_map/all_to_all | solution.py:338

commit v2 on v1

--- a/solution.py
+++ b/solution.py
@@ -43,39 +43,27 @@
     enc_ref[...] = (pre * jax.nn.sigmoid(pre)).astype(BF16)
 
 
-def pick_kernel(cells_ref, grad_ref, out_ref, grad_t):
-    blocks, width = cells_ref.shape
-    ncell, feats = grad_ref.shape
-    grad_t[...] = grad_ref[...].T
-
-    def body(i, _):
-        ids = lax.broadcasted_iota(jnp.int32, (ncell, width), 0)
-        match = (ids == cells_ref[pl.ds(i, 1), :]).astype(F32).astype(BF16)
-        out = dot(grad_t[...], match)
-        out_ref[pl.ds(pl.multiple_of(i * width, width), width), :] = out.T.astype(BF16)
-        return 0
-
-    lax.fori_loop(0, blocks, body, 0)
-
-
 def plan(n, need):
     unit = 16 * n
     units = -(-need // unit)
     streams = min(4, units)
-    sizes = [unit * (units // streams + (1 if i < units % streams else 0)) for i in range(streams)]
-    return sizes
+    marks = [units * i // streams for i in range(streams + 1)]
+    return [unit * (b - a) for a, b in zip(marks, marks[1:])]
 
 
 def conv_kernel(
-    n, sizes, xb, gb, w, pre_ref, mean_ref, denom_ref, ew_ref,
-    feat_ref, cell_ref, sum_ref,
-    xt, acc, denc, sbuf, rbuf, rs_send, rs_recv, ag_send, ag_recv,
+    n, sizes, xb, gb, w, pre_ref, mean_ref, denom_ref, ew_ref, cells_ref,
+    feat_ref, back_ref, sum_ref, scale_ref,
+    xt, acc, denc, sbuf, rbuf, cell_ref, grad_t, picked, squares,
+    rs_send, rs_recv, ag_send, ag_recv, ob_send, ob_recv,
 ):
     lane = xb.shape[2]
     lat16 = pre_ref.shape[0]
     cols = (xb.shape[1] - lat16) // 2
     feats = mean_ref.shape[1]
     taps = 9
+    blocks, width = cells_ref.shape
+    cap = picked.shape[0] // n
     me = lax.axis_index("lon")
     levels = n.bit_length() - 1
 
@@ -86,17 +74,21 @@
         return me + (1 - 2 * bit_of(k)) * (2**k)
 
     barrier = pltpu.get_barrier_semaphore()
-    for k in range(levels):
+
+    def greet(i, _):
         pl.semaphore_signal(
-            barrier, inc=1, device_id={"lon": partner(k)}, device_id_type=pl.DeviceIdType.MESH
+            barrier, inc=1, device_id={"lon": lax.rem(me + i, n)},
+            device_id_type=pl.DeviceIdType.MESH,
         )
-    pl.semaphore_wait(barrier, levels)
+        return 0
+
+    lax.fori_loop(1, n, greet, 0)
 
     starts, ranges = [], []
     base = 0
     for s, size in enumerate(sizes):
         order = list(range(levels))
-        if s % 2 and levels > 2:
+        if s % 2 == 0 and levels > 2:
             order = [0] + order[2:] + [1]
         off, length, stages = base, size, []
         for k in order:
@@ -139,6 +131,19 @@
         copy.start()
         copies.append(copy)
         flying[s] = copy
+
+    def add_squares(start, length):
+        value = sum_ref[pl.ds(start, length), :].astype(F32)
+        squares[...] += jnp.sum(value * value, axis=0, keepdims=True)
+
+    def gradient_copy(i):
+        peer = lax.rem(me + i, n)
+        return pltpu.make_async_remote_copy(
+            src_ref=picked.at[pl.ds(pl.multiple_of(peer * cap, 16), cap), :],
+            dst_ref=back_ref.at[pl.ds(pl.multiple_of(me * cap, 16), cap), :],
+            send_sem=ob_send.at[i], recv_sem=ob_recv.at[i],
+            device_id={"lon": peer}, device_id_type=pl.DeviceIdType.MESH,
+        )
 
     def begin(s):
         send_sum(s, 0)
@@ -157,14 +162,19 @@
             else:
                 sum_ref[pl.ds(keep, half), :] = value.astype(BF16)
                 send_result(s, levels - 1)
+                add_squares(keep, half)
         else:
             j = 2 * levels - 1 - p
             if j > 0:
                 send_result(s, j - 1)
+            k, keep, send, half = ranges[s][j]
+            add_squares(send, half)
         pos[s] = p + 1
 
+    squares[...] = jnp.zeros_like(squares)
     for b in range(3):
         xt[b] = xb[b, pl.ds(cols, lat16), :].T
+    pl.semaphore_wait(barrier, n - 1)
 
     def raw_tap(t, _):
         a, b = t // 3, lax.rem(t, 3)
@@ -209,8 +219,8 @@
         begin(s)
     if done < taps:
         lax.fori_loop(done, taps, raw_tap, 0)
-    for r in range(0, tiles, 2):
-        lax.fori_loop(r, min(r + 2, tiles), denc_tile, 0)
+    for r in range(tiles):
+        denc_tile(r, 0)
         for s in range(last):
             step(s)
     acc[taps * lane : taps * lane + feats, :] = lax.dot_general(
@@ -219,47 +229,81 @@
     if taps * lane + feats < base:
         acc[taps * lane + feats : base, :] = jnp.zeros((base - taps * lane - feats, lane), F32)
     begin(last)
-    for r in range(0, tiles, 2):
-        lax.fori_loop(r, min(r + 2, tiles), feat_tile, 0)
+
+    grad_t[...] = cell_ref[...].T
+
+    def pick(i, _):
+        ids = lax.broadcasted_iota(jnp.int32, (lat16, width), 0)
+        match = (ids == cells_ref[pl.ds(i, 1), :]).astype(F32).astype(BF16)
+        out = dot(grad_t[...], match)
+        picked[pl.ds(pl.multiple_of(i * width, width), width), :] = out.T.astype(BF16)
+        return 0
+
+    lax.fori_loop(0, blocks, pick, 0)
+
+    def send_gradient(i, _):
+        gradient_copy(i).start()
+        return 0
+
+    lax.fori_loop(1, n, send_gradient, 0)
+    own = pl.ds(pl.multiple_of(me * cap, 16), cap)
+    back_ref[own, :] = picked[own, :]
+    for r in range(tiles):
         for s in range(last + 1):
             step(s)
+        feat_tile(r, 0)
     while min(pos) < 2 * levels:
         for s in range(last + 1):
             step(s)
+    norm = jnp.sqrt(jnp.sum(squares[...], axis=1, keepdims=True))
+    scale_ref[...] = jnp.broadcast_to(jnp.minimum(1.0, 1.0 / (norm + 1e-06)), scale_ref.shape)
+
+    def finish_gradient(i, _):
+        gradient_copy(i).wait()
+        return 0
+
+    lax.fori_loop(1, n, finish_gradient, 0)
     for copy in copies:
         copy.wait_send()
 
 
-def conv_call(n, xb, gb, w, pre, mean, denom, ew):
+def conv_call(n, xb, gb, w, pre, mean, denom, ew, cells):
     lane = xb.shape[2]
     ncell, feats = mean.shape
     need = 9 * lane + feats
     sizes = plan(n, need)
     rows = sum(sizes)
     levels = n.bit_length() - 1
+    total = cells.shape[0] * cells.shape[1]
     sems = pltpu.SemaphoreType.DMA((len(sizes), levels))
     return pl.pallas_call(
         functools.partial(conv_kernel, n, sizes),
         out_shape=(
             jax.ShapeDtypeStruct((ncell, lane), BF16),
-            jax.ShapeDtypeStruct((ncell, feats), BF16),
+            jax.ShapeDtypeStruct((total, feats), BF16),
             jax.ShapeDtypeStruct((rows, lane), BF16),
+            jax.ShapeDtypeStruct((8, 128), F32),
         ),
-        in_specs=[VMEM] * 7,
-        out_specs=(VMEM,) * 3,
+        in_specs=[VMEM] * 8,
+        out_specs=(VMEM,) * 4,
         scratch_shapes=[
             pltpu.VMEM((3, lane, ncell), BF16),
             pltpu.VMEM((rows, lane), F32),
             pltpu.VMEM((ncell, lane), BF16),
             pltpu.VMEM((rows, lane), BF16),
             pltpu.VMEM((rows, lane), BF16),
+            pltpu.VMEM((ncell, feats), BF16),
+            pltpu.VMEM((feats, ncell), BF16),
+            pltpu.VMEM((total, feats), BF16),
+            pltpu.VMEM((1, lane), F32),
             sems, sems, sems, sems,
+            pltpu.SemaphoreType.DMA((n,)), pltpu.SemaphoreType.DMA((n,)),
         ],
         compiler_params=pltpu.CompilerParams(
             collective_id=0, has_side_effects=True, vmem_limit_bytes=LIMIT
         ),
         name="conv",
-    )(xb, gb, w, pre, mean, denom, ew)
+    )(xb, gb, w, pre, mean, denom, ew, cells)
 
 
 def shifted(grid, ntiles):
@@ -323,33 +367,21 @@
 
     gb = shifted(cotangent, ntiles)
     xb = shifted(encoded.reshape(lat_rows, lon_cols, chans), ntiles)
-    features, cell_grad, sums = conv_call(
-        ntiles, xb, gb, conv_weight.reshape(9 * chans, chans), pre, mean, denom, enc_weight
+    features, back_rows, sums, scale = conv_call(
+        ntiles, xb, gb, conv_weight.reshape(9 * chans, chans), pre, mean, denom, enc_weight,
+        recv_cells,
     )
-    slot_grads = pl.pallas_call(
-        pick_kernel,
-        out_shape=jax.ShapeDtypeStruct((total, feats), BF16),
-        in_specs=[VMEM] * 2,
-        out_specs=VMEM,
-        scratch_shapes=[pltpu.VMEM((feats, ncell), BF16)],
-        compiler_params=pltpu.CompilerParams(vmem_limit_bytes=LIMIT),
-        name="pick",
-    )(recv_cells, cell_grad)
-    back_rows = lax.all_to_all(
-        slot_grads.reshape(ntiles, cap, feats), "lon", split_axis=0, concat_axis=0, tiled=True
-    ).reshape(total, feats)
     take = (slot_of[:, None] == slots[None, :]).astype(BF16)
     obs_grad = dot(take, back_rows).astype(BF16)
 
-    sums = sums[: 9 * chans + feats].astype(F32)
-    norm = jnp.sqrt(jnp.sum(sums * sums))
-    scale = jnp.minimum(1.0, 1.0 / (norm + 1e-06))
-    out = (sums * scale).astype(BF16)
+    factor = scale[0, 0]
+    conv_out = (sums[: 9 * chans].astype(F32) * factor).astype(BF16)
+    enc_out = (sums[9 * chans : 9 * chans + feats].astype(F32) * factor).astype(BF16)
     return (
         features.reshape(cotangent.shape),
         obs_grad,
-        out[: 9 * chans].reshape(conv_weight.shape),
-        out[9 * chans :],
+        conv_out.reshape(conv_weight.shape),
+        enc_out,
     )
 
 

time: 137 us -> 136 us (level)
  Pallas kernels: 68.8 us -> 83.7 us
  waiting for transfers between devices: 23.1 us -> 13.4 us
  starting transfers between devices: 20.2 us -> 16.6 us
  local copies, waits for them, and re-layouts: 5.88 us -> 3.96 us
    pallas_call x1, Pallas kernels: 62.5 us -> 80.8 us  [conv_call(): pl.pallas_call(functools.partial(conv_kernel, n, sizes), out_shape=(jax.S...]
    all_to_all x1 -> x0, waiting for transfers between devices: 9.68 us -> none  [per_device(): lax.all_to_all(slot_grads.reshape(ntiles, cap, feats), 'lon', split_axis=...]
    convert_element_type x1 -> x2, other arithmetic: 2.32 us -> 6.61 us  [the longest x1 4.41 us: per_device(): conv_out = (sums[:9 * chans].astype(F32) * factor).astype(BF16)]
    reduce_sum x1 -> x0, other arithmetic: 3.8 us -> none  [per_device(): norm = jnp.sqrt(jnp.sum(sums * sums))]
    all_to_all x1 -> x0, starting transfers between devices: 3.57 us -> none  [per_device(): lax.all_to_all(slot_grads.reshape(ntiles, cap, feats), 'lon', split_axis=...]
    pallas_call x1 -> x0, Pallas kernels: 3.42 us -> none  [per_device(): pl.pallas_call(pick_kernel, out_shape=jax.ShapeDtypeStruct((total, feats)...]
    slice x2 -> x1, local copies, waits for them, and re-layouts: 2.42 us -> 0.51 us  [per_device(): factor = scale[0, 0]]
  transfers between devices with their start and end apart: 6 -> 5, of which waited for: 4 -> 3; matrix products, arithmetic and copies ran while one was open for 6% -> 3% of each run, Pallas kernels for 0% -> 0%
where the time goes in v2:
time: 136 us
  Pallas kernels  83.7 us (62%)
  starting transfers between devices  16.6 us (12%)
  waiting for transfers between devices  13.4 us (10%)
  other arithmetic  12.2 us (9%)
  matrix products  4.9 us (4%)
  local copies, waits for them, and re-layouts  3.96 us (3%)
    pallas_call x1, Pallas kernels, conv_call(): pl.pallas_call(functools.partial(conv_kernel, n, sizes), out_shape=(jax.S...  80.8 us
    ppermute x2, waiting for transfers between devices, shifted(): before = lax.ppermute(grid[:, -1:], 'lon', up)  13.3 us
    ppermute x2, starting transfers between devices, shifted(): after = lax.ppermute(grid[:, :1], 'lon', down)  8.7 us
    all_to_all x1, starting transfers between devices, per_device(): got = lax.all_to_all(block, 'lon', split_axis=0, concat_axis=0, tiled=True)  7.38 us
    dot_general x2, matrix products, dot(): return jnp.dot(a, b, preferred_element_type=F32)  4.9 us
    convert_element_type x1, other arithmetic, per_device(): conv_out = (sums[:9 * chans].astype(F32) * factor).astype(BF16)  4.41 us
    another operation x6, other arithmetic, shifted(): jnp.stack([jnp.concatenate([before, grid[:, :-1]], axis=1), grid, jnp.con...  3.09 us
    pallas_call x1, Pallas kernels, per_device(): pl.pallas_call(encode_kernel, out_shape=(jax.ShapeDtypeStruct((ncell, fea...  2.85 us
  transfers between devices with their start and end apart: 5, of which 3 were waited for; matrix products, arithmetic and copies ran while one was open for 3% of the time, Pallas kernels for 0%

profile of v2, /device:TPU:0, one launch (start us, length us, event | category | flops | bytes accessed | tf_op | source)
XLA Modules:
  0.0 135.6 jit_solution(803472704372388267)
XLA Ops:
  0.6 0.7 subtract_bitcast_fusion
  1.3 0.7 fusion.22
  2.0 0.7 copy.24
  2.8 0.1 reduce
  2.9 0.1 select_reduce_fusion
  3.0 0.2 stack.40
  3.2 0.2 stack.41
  3.4 0.1 pad.33.clone
  3.5 2.7 %fusion.5 = bf16[2048,256]{1,0:T(8,128)(2,1)S(1)} fusion(s32[1024]{0:T(1024)S(1)} %iota_add_fusion, bf16[1024,1]{1,0:T(8,128)(2,1)S(1)} %stack.41, bf16[1024,1]{1,0:T(8,128)(2,1)S(1)} %stack.40, bf16[1024,128]{1,0:T(8,128)(2,1)} %param.6, bf16[256]{0:T(256)(128)(2,1)S(1)} %pad.33.clone), kind=kOutput, calls=%fused_computation.10 | convolution fusion | flops 1078460416 | bytes 1319424 | tf_op jit(solution)/shard_map/dot_general | solution.py:16
  6.2 0.0 copy-start.1
  6.3 0.2 copy.27
  6.5 0.9 fusion.9
  7.4 7.4 %all-to-all-start = ((bf16[16,144,128]{2,1,0:T(8,128)(2,1)}), bf16[16,144,128]{2,1,0:T(8,128)(2,1)S(1)}, u32[]{:S(2)}, u32[]{:S(2)}) async-start(bf16[16,144,128]{2,1,0:T(8,128)(2,1)} %fusion.9), calls=%async_computation | async-start | bytes 1179648 | tf_op jit(solution)/shard_map/all_to_all | solution.py:346
  14.8 0.0 copy-done.1
  14.8 0.2 fusion.27
  15.0 0.5 collective-permute-start.2
  15.4 4.0 %collective-permute-start.3 = (bf16[64,1,384]{2,1,0:T(2,128)(2,1)S(1)}, bf16[64,1,384]{2,1,0:T(2,128)(2,1)S(1)}, u32[]{:S(2)}, u32[]{:S(2)}) collective-permute-start(bf16[64,1,384]{2,1,0:T(2,128)(2,1)S(1)} %get-tuple-element.21), channel_id=1, source_target_pairs={{1,0},{2,1},{3,2},{4,3},{5,4},{6,5},{7,6},{8,7},{9,8},{10,9},{11,1... | collective-permute-start | bytes 147464 | tf_op jit(solution)/shard_map/ppermute | solution.py:313
  19.5 0.3 fusion.28
  19.8 11.6 %collective-permute-done.2 = bf16[64,1,384]{2,1,0:T(2,128)(2,1)S(1)} collective-permute-done((bf16[64,1,384]{2,1,0:T(2,128)(2,1)S(1)}, bf16[64,1,384]{2,1,0:T(2,128)(2,1)S(1)}, u32[]{:S(2)}, u32[]{:S(2)}) %collective-permute-start.2) | collective-permute-done | bytes 49184 | tf_op jit(solution)/shard_map/ppermute | solution.py:312
  31.4 0.4 maximum_bitcast_fusion.2
  31.7 0.0 collective-permute-done.3
  31.7 0.2 maximum_bitcast_fusion.3
  32.0 0.0 copy-start
  32.0 1.6 %select_maximum_fusion = bf16[3,66,16,384]{3,2,1,0:T(8,128)(2,1)} fusion(bf16[1,64,16,384]{3,2,1,0:T(8,128)(2,1)S(1)} %maximum_bitcast_fusion.3, bf16[1,64,16,384]{3,2,1,0:T(8,128)(2,1)S(1)} %bitcast.32, bf16[1,64,16,384]{3,2,1,0:T(8,128)(2,1)S(1)} %maximum_bitcast_fusion.2), kind=kLoop, calls=%fused_computation.11 | loop fusion | flops 14598144 | bytes 4792320 | tf_op jit(solution)/shard_map/stack | solution.py:314
  33.6 0.0 all-to-all-done
  33.7 0.0 copy-done
  33.7 2.8 %encode.1 = (bf16[1024,128]{1,0:T(8,128)(2,1)S(1)}, f32[1024,128]{1,0:T(8,128)S(1)}, f32[1024,384]{1,0:T(8,128)S(1)}, bf16[1024,384]{1,0:T(8,128)(2,1)S(1)}) custom-call(s32[8,256]{1,0:T(8,128)S(1)} %add.42.cells_ref, bf16[2048,128]{1,0:T(8,128)(2,1)S(1)} %bitcast.29, bf16[128,384]{1,0:T(8,128)(2,1)S(1)} %copy-done), custom_call_target="tpu_custom_call" | custom-call | tf_op jit(solution)/shard_map/encode/pallas_call | solution.py:353
  36.6 0.2 fusion.29
  36.7 0.1 collective-permute-start
  36.8 0.3 fusion.30
  37.2 4.7 %collective-permute-start.1 = (bf16[64,1,384]{2,1,0:T(2,128)(2,1)S(1)}, bf16[64,1,384]{2,1,0:T(2,128)(2,1)S(1)}, u32[]{:S(2)}, u32[]{:S(2)}) collective-permute-start(bf16[64,1,384]{2,1,0:T(2,128)(2,1)S(1)} %get-tuple-element.25), channel_id=1, source_target_pairs={{1,0},{2,1},{3,2},{4,3},{5,4},{6,5},{7,6},{8,7},{9,8},{10,9},{11,1... | collective-permute-start | bytes 147464 | tf_op jit(solution)/shard_map/ppermute | solution.py:313
  41.8 1.7 %collective-permute-done = bf16[64,1,384]{2,1,0:T(2,128)(2,1)S(1)} collective-permute-done((bf16[64,1,384]{2,1,0:T(2,128)(2,1)S(1)}, bf16[64,1,384]{2,1,0:T(2,128)(2,1)S(1)}, u32[]{:S(2)}, u32[]{:S(2)}) %collective-permute-start) | collective-permute-done | bytes 49184 | tf_op jit(solution)/shard_map/ppermute | solution.py:312
  43.5 0.4 maximum_bitcast_fusion
  43.9 0.1 collective-permute-done.1
  44.0 0.3 maximum_bitcast_fusion.1
  44.3 0.3 select_maximum_fusion.2
  44.6 80.8 %conv.1 = (bf16[1024,384]{1,0:T(8,128)(2,1)S(1)}, bf16[2048,128]{1,0:T(8,128)(2,1)S(1)}, bf16[3584,384]{1,0:T(8,128)(2,1)}, f32[8,128]{1,0:T(8,128)S(1)}) custom-call(bf16[3,1056,384]{2,1,0:T(8,128)(2,1)S(1)} %bitcast.25, bf16[3,1056,384]{2,1,0:T(8,128)(2,1)} %bitcast.31, bf16[3456,384]{1,0:T(8,128)(2,1)} %bitcast.34, ...), custom_call_target="tpu_custom_call" | custom-call | tf_op jit(solution)/shard_map/conv/pallas_call | solution.py:279
  125.4 0.5 slice.62
  125.9 2.2 %multiply_convert_fusion.1 = bf16[128,384]{1,0:T(8,128)(2,1)} fusion(f32[]{:T(128)} %bitcast.17, bf16[3584,384]{1,0:T(8,128)(2,1)} %get-tuple-element.18), kind=kLoop, calls=%fused_computation.31 | loop fusion | flops 147456 | bytes 196612 | tf_op jit(solution)/shard_map/convert_element_type | solution.py:379
  128.1 4.4 %multiply_convert_fusion = bf16[3456,384]{1,0:T(8,128)(2,1)} fusion(f32[]{:T(128)} %bitcast.17, bf16[3584,384]{1,0:T(8,128)(2,1)} %get-tuple-element.18), kind=kLoop, calls=%fused_computation.6 | loop fusion | flops 3981312 | bytes 5308420 | tf_op jit(solution)/shard_map/convert_element_type | solution.py:378
  132.5 2.2 %fusion.7 = bf16[1024,128]{1,0:T(8,128)(2,1)} fusion(bf16[2048,128]{1,0:T(8,128)(2,1)S(1)} %get-tuple-element.17, s32[1024]{0:T(1024)S(1)} %iota_add_fusion), kind=kOutput, calls=%fused_computation.16 | convolution fusion | flops 539099136 | bytes 790528 | tf_op jit(solution)/shard_map/dot_general | solution.py:16
  134.7 0.9 copy.29
  (8 shorter events, 0.2 us)
Async XLA Ops:
  6.2 8.6 %copy-start.1 = (bf16[64,16,384]{2,1,0:T(8,128)(2,1)S(1)}, bf16[64,16,384]{2,1,0:T(8,128)(2,1)}, u32[]{:S(2)}) copy-start(bf16[64,16,384]{2,1,0:T(8,128)(2,1)} %param.11) | copy-start | bytes 2359300
  7.4 26.2 %all-to-all-start = ((bf16[16,144,128]{2,1,0:T(8,128)(2,1)}), bf16[16,144,128]{2,1,0:T(8,128)(2,1)S(1)}, u32[]{:S(2)}, u32[]{:S(2)}) async-start(bf16[16,144,128]{2,1,0:T(8,128)(2,1)} %fusion.9), calls=%async_computation | async-start | bytes 1179648 | tf_op jit(solution)/shard_map/all_to_all | solution.py:346
  15.0 16.4 %collective-permute-start.2 = (bf16[64,1,384]{2,1,0:T(2,128)(2,1)S(1)}, bf16[64,1,384]{2,1,0:T(2,128)(2,1)S(1)}, u32[]{:S(2)}, u32[]{:S(2)}) collective-permute-start(bf16[64,1,384]{2,1,0:T(2,128)(2,1)S(1)} %get-tuple-element.20), channel_id=1, source_target_pairs={{0,1},{1,2},{2,3},{3,4},{4,5},{5,6},{6,7},{7,8},{8,9},{9,10},{10,1... | collective-permute-start | bytes 147464 | tf_op jit(solution)/shard_map/ppermute | solution.py:312
  15.4 16.3 %collective-permute-start.3 = (bf16[64,1,384]{2,1,0:T(2,128)(2,1)S(1)}, bf16[64,1,384]{2,1,0:T(2,128)(2,1)S(1)}, u32[]{:S(2)}, u32[]{:S(2)}) collective-permute-start(bf16[64,1,384]{2,1,0:T(2,128)(2,1)S(1)} %get-tuple-element.21), channel_id=1, source_target_pairs={{1,0},{2,1},{3,2},{4,3},{5,4},{6,5},{7,6},{8,7},{9,8},{10,9},{11,1... | collective-permute-start | bytes 147464 | tf_op jit(solution)/shard_map/ppermute | solution.py:313
  32.0 1.7 %copy-start = (bf16[128,384]{1,0:T(8,128)(2,1)S(1)}, bf16[128,384]{1,0:T(8,128)(2,1)}, u32[]{:S(2)}) copy-start(bf16[128,384]{1,0:T(8,128)(2,1)} %ew_ref.1) | copy-start | bytes 294916
  36.7 6.8 %collective-permute-start = (bf16[64,1,384]{2,1,0:T(2,128)(2,1)S(1)}, bf16[64,1,384]{2,1,0:T(2,128)(2,1)S(1)}, u32[]{:S(2)}, u32[]{:S(2)}) collective-permute-start(bf16[64,1,384]{2,1,0:T(2,128)(2,1)S(1)} %get-tuple-element.24), channel_id=1, source_target_pairs={{0,1},{1,2},{2,3},{3,4},{4,5},{5,6},{6,7},{7,8},{8,9},{9,10},{10,1... | collective-permute-start | bytes 147464 | tf_op jit(solution)/shard_map/ppermute | solution.py:312
  37.2 6.9 %collective-permute-start.1 = (bf16[64,1,384]{2,1,0:T(2,128)(2,1)S(1)}, bf16[64,1,384]{2,1,0:T(2,128)(2,1)S(1)}, u32[]{:S(2)}, u32[]{:S(2)}) collective-permute-start(bf16[64,1,384]{2,1,0:T(2,128)(2,1)S(1)} %get-tuple-element.25), channel_id=1, source_target_pairs={{1,0},{2,1},{3,2},{4,3},{5,4},{6,5},{7,6},{8,7},{9,8},{10,9},{11,1... | collective-permute-start | bytes 147464 | tf_op jit(solution)/shard_map/ppermute | solution.py:313

commit v3 on v2

--- a/solution.py
+++ b/solution.py
@@ -46,7 +46,7 @@
 def plan(n, need):
     unit = 16 * n
     units = -(-need // unit)
-    streams = min(4, units)
+    streams = min(7, units)
     marks = [units * i // streams for i in range(streams + 1)]
     return [unit * (b - a) for a, b in zip(marks, marks[1:])]
 
@@ -88,7 +88,7 @@
     base = 0
     for s, size in enumerate(sizes):
         order = list(range(levels))
-        if s % 2 == 0 and levels > 2:
+        if s % 3 == 1 and levels > 2:
             order = [0] + order[2:] + [1]
         off, length, stages = base, size, []
         for k in order:

time: 136 us -> 130 us (0.956)
  Pallas kernels: 83.7 us -> 77 us
    pallas_call x1, Pallas kernels: 80.8 us -> 74.2 us  [conv_call(): pl.pallas_call(functools.partial(conv_kernel, n, sizes), out_shape=(jax.S...]
where the time goes in v3:
time: 130 us; the launch traced here: 129 us
  Pallas kernels  77 us (59%)
  starting transfers between devices  16.6 us (13%)
  waiting for transfers between devices  13.4 us (10%)
  other arithmetic  12.2 us (9%)
  matrix products  4.9 us (4%)
  local copies, waits for them, and re-layouts  3.96 us (3%)
    pallas_call x1, Pallas kernels, conv_call(): pl.pallas_call(functools.partial(conv_kernel, n, sizes), out_shape=(jax.S...  74.2 us
    ppermute x2, waiting for transfers between devices, shifted(): before = lax.ppermute(grid[:, -1:], 'lon', up)  13.3 us
    ppermute x2, starting transfers between devices, shifted(): after = lax.ppermute(grid[:, :1], 'lon', down)  8.7 us
    all_to_all x1, starting transfers between devices, per_device(): got = lax.all_to_all(block, 'lon', split_axis=0, concat_axis=0, tiled=True)  7.38 us
    dot_general x2, matrix products, dot(): return jnp.dot(a, b, preferred_element_type=F32)  4.9 us
    convert_element_type x1, other arithmetic, per_device(): conv_out = (sums[:9 * chans].astype(F32) * factor).astype(BF16)  4.41 us
    another operation x6, other arithmetic, shifted(): jnp.stack([jnp.concatenate([before, grid[:, :-1]], axis=1), grid, jnp.con...  3.09 us
    pallas_call x1, Pallas kernels, per_device(): pl.pallas_call(encode_kernel, out_shape=(jax.ShapeDtypeStruct((ncell, fea...  2.85 us
  transfers between devices with their start and end apart: 5, of which 3 were waited for; matrix products, arithmetic and copies ran while one was open for 3% of the time, Pallas kernels for 0%

profile of v3, /device:TPU:0, one launch (start us, length us, event | category | flops | bytes accessed | tf_op | source)
XLA Modules:
  0.0 129.0 jit_solution(2390124994973139037)
XLA Ops:
  0.6 0.7 subtract_bitcast_fusion
  1.3 0.7 fusion.22
  2.0 0.7 copy.24
  2.8 0.1 reduce
  2.9 0.1 select_reduce_fusion
  3.0 0.2 stack.40
  3.2 0.2 stack.41
  3.4 0.1 pad.33.clone
  3.5 2.7 %fusion.5 = bf16[2048,256]{1,0:T(8,128)(2,1)S(1)} fusion(s32[1024]{0:T(1024)S(1)} %iota_add_fusion, bf16[1024,1]{1,0:T(8,128)(2,1)S(1)} %stack.41, bf16[1024,1]{1,0:T(8,128)(2,1)S(1)} %stack.40, bf16[1024,128]{1,0:T(8,128)(2,1)} %param.6, bf16[256]{0:T(256)(128)(2,1)S(1)} %pad.33.clone), kind=kOutput, calls=%fused_computation.10 | convolution fusion | flops 1078460416 | bytes 1319424 | tf_op jit(solution)/shard_map/dot_general | solution.py:16
  6.2 0.0 copy-start.1
  6.3 0.2 copy.27
  6.5 0.9 fusion.9
  7.4 7.4 %all-to-all-start = ((bf16[16,144,128]{2,1,0:T(8,128)(2,1)}), bf16[16,144,128]{2,1,0:T(8,128)(2,1)S(1)}, u32[]{:S(2)}, u32[]{:S(2)}) async-start(bf16[16,144,128]{2,1,0:T(8,128)(2,1)} %fusion.9), calls=%async_computation | async-start | bytes 1179648 | tf_op jit(solution)/shard_map/all_to_all | solution.py:346
  14.8 0.0 copy-done.1
  14.8 0.2 fusion.27
  15.0 0.5 collective-permute-start.2
  15.4 4.0 %collective-permute-start.3 = (bf16[64,1,384]{2,1,0:T(2,128)(2,1)S(1)}, bf16[64,1,384]{2,1,0:T(2,128)(2,1)S(1)}, u32[]{:S(2)}, u32[]{:S(2)}) collective-permute-start(bf16[64,1,384]{2,1,0:T(2,128)(2,1)S(1)} %get-tuple-element.21), channel_id=1, source_target_pairs={{1,0},{2,1},{3,2},{4,3},{5,4},{6,5},{7,6},{8,7},{9,8},{10,9},{11,1... | collective-permute-start | bytes 147464 | tf_op jit(solution)/shard_map/ppermute | solution.py:313
  19.5 0.3 fusion.28
  19.8 11.6 %collective-permute-done.2 = bf16[64,1,384]{2,1,0:T(2,128)(2,1)S(1)} collective-permute-done((bf16[64,1,384]{2,1,0:T(2,128)(2,1)S(1)}, bf16[64,1,384]{2,1,0:T(2,128)(2,1)S(1)}, u32[]{:S(2)}, u32[]{:S(2)}) %collective-permute-start.2) | collective-permute-done | bytes 49184 | tf_op jit(solution)/shard_map/ppermute | solution.py:312
  31.4 0.4 maximum_bitcast_fusion.2
  31.7 0.0 collective-permute-done.3
  31.7 0.2 maximum_bitcast_fusion.3
  32.0 0.0 copy-start
  32.0 1.6 %select_maximum_fusion = bf16[3,66,16,384]{3,2,1,0:T(8,128)(2,1)} fusion(bf16[1,64,16,384]{3,2,1,0:T(8,128)(2,1)S(1)} %maximum_bitcast_fusion.3, bf16[1,64,16,384]{3,2,1,0:T(8,128)(2,1)S(1)} %bitcast.32, bf16[1,64,16,384]{3,2,1,0:T(8,128)(2,1)S(1)} %maximum_bitcast_fusion.2), kind=kLoop, calls=%fused_computation.11 | loop fusion | flops 14598144 | bytes 4792320 | tf_op jit(solution)/shard_map/stack | solution.py:314
  33.6 0.0 all-to-all-done
  33.7 0.0 copy-done
  33.7 2.8 %encode.1 = (bf16[1024,128]{1,0:T(8,128)(2,1)S(1)}, f32[1024,128]{1,0:T(8,128)S(1)}, f32[1024,384]{1,0:T(8,128)S(1)}, bf16[1024,384]{1,0:T(8,128)(2,1)S(1)}) custom-call(s32[8,256]{1,0:T(8,128)S(1)} %add.42.cells_ref, bf16[2048,128]{1,0:T(8,128)(2,1)S(1)} %bitcast.29, bf16[128,384]{1,0:T(8,128)(2,1)S(1)} %copy-done), custom_call_target="tpu_custom_call" | custom-call | tf_op jit(solution)/shard_map/encode/pallas_call | solution.py:353
  36.6 0.2 fusion.29
  36.7 0.1 collective-permute-start
  36.8 0.3 fusion.30
  37.2 4.7 %collective-permute-start.1 = (bf16[64,1,384]{2,1,0:T(2,128)(2,1)S(1)}, bf16[64,1,384]{2,1,0:T(2,128)(2,1)S(1)}, u32[]{:S(2)}, u32[]{:S(2)}) collective-permute-start(bf16[64,1,384]{2,1,0:T(2,128)(2,1)S(1)} %get-tuple-element.25), channel_id=1, source_target_pairs={{1,0},{2,1},{3,2},{4,3},{5,4},{6,5},{7,6},{8,7},{9,8},{10,9},{11,1... | collective-permute-start | bytes 147464 | tf_op jit(solution)/shard_map/ppermute | solution.py:313
  41.8 1.7 %collective-permute-done = bf16[64,1,384]{2,1,0:T(2,128)(2,1)S(1)} collective-permute-done((bf16[64,1,384]{2,1,0:T(2,128)(2,1)S(1)}, bf16[64,1,384]{2,1,0:T(2,128)(2,1)S(1)}, u32[]{:S(2)}, u32[]{:S(2)}) %collective-permute-start) | collective-permute-done | bytes 49184 | tf_op jit(solution)/shard_map/ppermute | solution.py:312
  43.5 0.4 maximum_bitcast_fusion
  43.9 0.1 collective-permute-done.1
  44.0 0.3 maximum_bitcast_fusion.1
  44.3 0.3 select_maximum_fusion.2
  44.6 74.2 %conv.1 = (bf16[1024,384]{1,0:T(8,128)(2,1)S(1)}, bf16[2048,128]{1,0:T(8,128)(2,1)S(1)}, bf16[3584,384]{1,0:T(8,128)(2,1)}, f32[8,128]{1,0:T(8,128)S(1)}) custom-call(bf16[3,1056,384]{2,1,0:T(8,128)(2,1)S(1)} %bitcast.25, bf16[3,1056,384]{2,1,0:T(8,128)(2,1)} %bitcast.31, bf16[3456,384]{1,0:T(8,128)(2,1)} %bitcast.34, ...), custom_call_target="tpu_custom_call" | custom-call | tf_op jit(solution)/shard_map/conv/pallas_call | solution.py:279
  118.8 0.5 slice.62
  119.3 2.2 %multiply_convert_fusion.1 = bf16[128,384]{1,0:T(8,128)(2,1)} fusion(f32[]{:T(128)} %bitcast.17, bf16[3584,384]{1,0:T(8,128)(2,1)} %get-tuple-element.18), kind=kLoop, calls=%fused_computation.31 | loop fusion | flops 147456 | bytes 196612 | tf_op jit(solution)/shard_map/convert_element_type | solution.py:379
  121.5 4.4 %multiply_convert_fusion = bf16[3456,384]{1,0:T(8,128)(2,1)} fusion(f32[]{:T(128)} %bitcast.17, bf16[3584,384]{1,0:T(8,128)(2,1)} %get-tuple-element.18), kind=kLoop, calls=%fused_computation.6 | loop fusion | flops 3981312 | bytes 5308420 | tf_op jit(solution)/shard_map/convert_element_type | solution.py:378
  125.9 2.2 %fusion.7 = bf16[1024,128]{1,0:T(8,128)(2,1)} fusion(bf16[2048,128]{1,0:T(8,128)(2,1)S(1)} %get-tuple-element.17, s32[1024]{0:T(1024)S(1)} %iota_add_fusion), kind=kOutput, calls=%fused_computation.16 | convolution fusion | flops 539099136 | bytes 790528 | tf_op jit(solution)/shard_map/dot_general | solution.py:16
  128.1 0.9 copy.29
  (8 shorter events, 0.2 us)
Async XLA Ops:
  6.2 8.6 %copy-start.1 = (bf16[64,16,384]{2,1,0:T(8,128)(2,1)S(1)}, bf16[64,16,384]{2,1,0:T(8,128)(2,1)}, u32[]{:S(2)}) copy-start(bf16[64,16,384]{2,1,0:T(8,128)(2,1)} %param.11) | copy-start | bytes 2359300
  7.4 26.2 %all-to-all-start = ((bf16[16,144,128]{2,1,0:T(8,128)(2,1)}), bf16[16,144,128]{2,1,0:T(8,128)(2,1)S(1)}, u32[]{:S(2)}, u32[]{:S(2)}) async-start(bf16[16,144,128]{2,1,0:T(8,128)(2,1)} %fusion.9), calls=%async_computation | async-start | bytes 1179648 | tf_op jit(solution)/shard_map/all_to_all | solution.py:346
  15.0 16.4 %collective-permute-start.2 = (bf16[64,1,384]{2,1,0:T(2,128)(2,1)S(1)}, bf16[64,1,384]{2,1,0:T(2,128)(2,1)S(1)}, u32[]{:S(2)}, u32[]{:S(2)}) collective-permute-start(bf16[64,1,384]{2,1,0:T(2,128)(2,1)S(1)} %get-tuple-element.20), channel_id=1, source_target_pairs={{0,1},{1,2},{2,3},{3,4},{4,5},{5,6},{6,7},{7,8},{8,9},{9,10},{10,1... | collective-permute-start | bytes 147464 | tf_op jit(solution)/shard_map/ppermute | solution.py:312
  15.4 16.3 %collective-permute-start.3 = (bf16[64,1,384]{2,1,0:T(2,128)(2,1)S(1)}, bf16[64,1,384]{2,1,0:T(2,128)(2,1)S(1)}, u32[]{:S(2)}, u32[]{:S(2)}) collective-permute-start(bf16[64,1,384]{2,1,0:T(2,128)(2,1)S(1)} %get-tuple-element.21), channel_id=1, source_target_pairs={{1,0},{2,1},{3,2},{4,3},{5,4},{6,5},{7,6},{8,7},{9,8},{10,9},{11,1... | collective-permute-start | bytes 147464 | tf_op jit(solution)/shard_map/ppermute | solution.py:313
  32.0 1.7 %copy-start = (bf16[128,384]{1,0:T(8,128)(2,1)S(1)}, bf16[128,384]{1,0:T(8,128)(2,1)}, u32[]{:S(2)}) copy-start(bf16[128,384]{1,0:T(8,128)(2,1)} %ew_ref.1) | copy-start | bytes 294916
  36.7 6.8 %collective-permute-start = (bf16[64,1,384]{2,1,0:T(2,128)(2,1)S(1)}, bf16[64,1,384]{2,1,0:T(2,128)(2,1)S(1)}, u32[]{:S(2)}, u32[]{:S(2)}) collective-permute-start(bf16[64,1,384]{2,1,0:T(2,128)(2,1)S(1)} %get-tuple-element.24), channel_id=1, source_target_pairs={{0,1},{1,2},{2,3},{3,4},{4,5},{5,6},{6,7},{7,8},{8,9},{9,10},{10,1... | collective-permute-start | bytes 147464 | tf_op jit(solution)/shard_map/ppermute | solution.py:312
  37.2 6.9 %collective-permute-start.1 = (bf16[64,1,384]{2,1,0:T(2,128)(2,1)S(1)}, bf16[64,1,384]{2,1,0:T(2,128)(2,1)S(1)}, u32[]{:S(2)}, u32[]{:S(2)}) collective-permute-start(bf16[64,1,384]{2,1,0:T(2,128)(2,1)S(1)} %get-tuple-element.25), channel_id=1, source_target_pairs={{1,0},{2,1},{3,2},{4,3},{5,4},{6,5},{7,6},{8,7},{9,8},{10,9},{11,1... | collective-permute-start | bytes 147464 | tf_op jit(solution)/shard_map/ppermute | solution.py:313
